TPU v7x, 32 devices: a whole 2x2x4 slice. The times are simulated.
32 devices in a mesh: sector: 8 (over y, x, core), op: 4 (over z).
Axes of the slice: x: 2, y: 2, z: 4, core: 2. Of those that a mesh axis runs over, the one named last changes fastest.
Arguments:
- theta: float32 [32, 128, 128], P('sector'), may hold values from -6 to 6
- left_env: bfloat16 [32, 64, 128, 128], P('sector', 'op'), may hold values from -3 to 3
- right_env: bfloat16 [32, 64, 128, 128], P('sector', 'op'), may hold values from -3 to 3
- perm: int32 [32], replicated, may hold values from 0 to 31, each once
- dims: int32 [32, 2], P('sector'), may hold values from 32 to 128, as said below
Outputs:
- lanczos_vec: float32 [32, 128, 128], P('sector')
- coeffs: float32 [6], replicated
- density: float32 [32, 128, 128], P('sector')
Inputs may be any that keep to these rules, and one draw needn't show every extreme that they name: `dims`: each entry is a kept dimension of 32 to 128; the first position has 128 on both sides.
All inputs are finite; a program needn't handle non-finite values.
Results may differ from a plain program's by a relative error of at most 0.012.
Values may be sent and summed in bfloat16 or wider, within the bound.
A program may use at most 64 MiB of HBM per device.

v0:
```python
import jax
import jax.numpy as jnp
from jax import lax
from jax.sharding import PartitionSpec as P


def local_mask(dims, row_count, width):
    rows = jnp.arange(row_count, dtype=jnp.int32)
    cols = jnp.arange(width, dtype=jnp.int32)
    inside_rows = (rows[None, :] < dims[:, 0:1]).astype(jnp.float32)
    inside_cols = (cols[None, :] < dims[:, 1:2]).astype(jnp.float32)
    return inside_rows[:, :, None] * inside_cols[:, None, :]


def neighbour_positions(perm, sec_dev):
    total = perm.shape[0]
    pos_of = jnp.argsort(perm)
    first = lax.axis_index("sector") * sec_dev
    mine = lax.dynamic_slice_in_dim(perm, first, sec_dev, 0)
    shifts = jnp.arange(3, dtype=jnp.int32) - 1
    return pos_of[(mine[:, None] + shifts[None, :]) % total].reshape(-1)


def pick_blocks(src_flat):

    def fold_fn(carry, piece, start):
        count = piece.shape[0]
        hits = (src_flat[:, None] == jnp.arange(count, dtype=jnp.int32)[None, :]).astype(
            jnp.bfloat16
        )
        return jnp.dot(hits, piece.reshape(count, -1), preferred_element_type=jnp.float32)

    return fold_fn


def term_products(nbrs, left_env, right_env):
    term_dev = left_env.shape[1]
    global_terms = lax.axis_index("op") * term_dev + jnp.arange(term_dev, dtype=jnp.int32)
    selector = jax.nn.one_hot(global_terms % 3, 3, dtype=jnp.bfloat16)
    picked = jnp.einsum("wq,pqjk->pwjk", selector, nbrs, preferred_element_type=jnp.float32).astype(
        jnp.bfloat16
    )
    inner = jnp.einsum(
        "pwij,pwjk->pwik", left_env, picked, preferred_element_type=jnp.float32
    ).astype(jnp.bfloat16)
    return jnp.einsum("pwik,pwkl->pil", inner, right_env, preferred_element_type=jnp.float32)


def per_device(theta, left_env, right_env, perm, dims):
    sec_dev, width, _ = theta.shape
    n_op = lax.axis_size("op")
    terms_all = left_env.shape[1] * n_op
    count = jnp.float32(lax.axis_size("sector") * sec_dev * width * width)
    scale = 1.0 / jnp.sqrt(jnp.float32(terms_all))
    src_flat = neighbour_positions(perm, sec_dev)
    fold_fn = pick_blocks(src_flat)
    mask = local_mask(dims, width, width)

    def sq_sum(first):
        return lax.psum(jnp.sum(first * first), "sector")

    start_vec = theta * mask
    vector = start_vec / jnp.sqrt(sq_sum(start_vec) / count + 1e-06)
    previous = jnp.zeros_like(vector)
    beta = jnp.float32(0.0)
    alphas = []
    betas = []
    for step in range(3):
        empty = jnp.zeros((sec_dev * 3, width * width), jnp.float32)
        carry = fold_fn(
            empty,
            lax.all_gather(vector.astype(jnp.bfloat16), "sector", axis=0, tiled=True),
            jnp.int32(0),
        )
        nbrs = carry.astype(jnp.bfloat16).reshape(sec_dev, 3, width, width)
        partial_sum = term_products(nbrs, left_env, right_env)
        image = lax.psum(partial_sum, "op") * scale * mask
        alpha = lax.psum(jnp.sum(vector * image), "sector") / count
        resid = image - alpha * vector - beta * previous
        beta_next = jnp.sqrt(sq_sum(resid) / count + 1e-06)
        beta = beta_next
        previous, vector = (vector, resid / beta)
        alphas.append(alpha)
        betas.append(beta)
    coeffs = jnp.stack(alphas + betas)
    density = jnp.einsum("pij,pkj->pik", vector, vector, precision=lax.Precision.HIGHEST) / width
    return (vector, coeffs, density)


def solution(mesh):
    placed = (
        P("sector", None, None),
        P("sector", "op", None, None),
        P("sector", "op", None, None),
        P(),
        P("sector", None),
    )
    return jax.shard_map(
        per_device,
        mesh=mesh,
        in_specs=placed,
        out_specs=(P("sector", None, None), P(), P("sector", None, None)),
        check_vma=False,
    )
```

profile of v0, /device:TPU:0, one launch (start us, length us, event | category | flops | bytes accessed | tf_op | source)
XLA Modules:
  0.0 330.6 jit_solution(2217269925982204087)
XLA Ops:
  8.1 1.7 multiply_reduce_fusion.6
  9.8 15.7 %psum.70 = f32[]{:T(128)} all-reduce(f32[]{:T(128)} %multiply_reduce_fusion.6), channel_id=1, replica_groups=mesh['sector'=8,'op'=4] {'sector'}, use_global_device_ids=true, to_apply=%region_2.3 | all-reduce | flops 1 | bytes 8 | tf_op jit(solution)/shard_map/psum | solution.py:60
  26.3 1.7 fusion.63
  28.8 2.3 sort.17
  31.9 19.1 %all-gather.4.cloned.1.call-done = bf16[32,128,128]{2,1,0:T(8,128)(2,1)} async-done(((bf16[4,128,128]{2,1,0:T(8,128)(2,1)}), bf16[32,128,128]{2,1,0:T(8,128)(2,1)}) %all-gather.4.cloned.1.call-update) | async-done | bytes 1048592 | tf_op jit(solution)/shard_map/all_gather | solution.py:72
  51.1 1.9 convolution_convert_fusion.2
  53.1 2.1 convert_bitcast_fusion.2
  55.2 5.0 %fusion.27 = f32[4,128,128]{2,1,0:T(8,128)} fusion(bf16[4,16,128,128]{3,2,1,0:T(8,128)(2,1)S(1)} %copy-done, bf16[4,16,128,128]{3,2,1,0:T(8,128)(2,1)} %param.6, bf16[4,16,128,128]{3,1,2,0:T(8,128)(2,1)} %convert_bitcast_fusion.2), kind=kOutput, calls=%fused_computation.22 | convolution fusion | flops 537919488 | bytes 6553600 | tf_op jit(solution)/shard_map/pwik,pwkl->pil/dot_general | solution.py:46
  60.3 35.4 %all-reduce.4.cloned.1.call-done = f32[4,128,128]{2,1,0:T(8,128)} async-done(((f32[4,128,128]{2,1,0:T(8,128)}), f32[4,128,128]{2,1,0:T(8,128)}) %all-reduce.4.cloned.1.call-update) | async-done | bytes 262160 | tf_op jit(solution)/shard_map/psum | solution.py:77
  95.8 1.7 multiply_reduce_fusion.5
  97.5 12.8 %psum.72 = f32[]{:T(128)} all-reduce(f32[]{:T(128)} %multiply_reduce_fusion.5), channel_id=1, replica_groups=mesh['sector'=8,'op'=4] {'sector'}, use_global_device_ids=true, to_apply=%region_5.6 | all-reduce | flops 1 | bytes 8 | tf_op jit(solution)/shard_map/psum | solution.py:78
  111.0 1.7 multiply_reduce_fusion.4
  112.7 12.4 %psum.73 = f32[]{:T(128)} all-reduce(f32[]{:T(128)} %multiply_reduce_fusion.4), channel_id=1, replica_groups=mesh['sector'=8,'op'=4] {'sector'}, use_global_device_ids=true, to_apply=%region_7.8 | all-reduce | flops 1 | bytes 8 | tf_op jit(solution)/shard_map/psum | solution.py:60
  125.8 1.8 fusion.64
  127.6 22.0 %all-gather.6.cloned.1.call-done = bf16[32,128,128]{2,1,0:T(8,128)(2,1)} async-done(((bf16[4,128,128]{2,1,0:T(8,128)(2,1)}), bf16[32,128,128]{2,1,0:T(8,128)(2,1)}) %all-gather.6.cloned.1.call-update) | async-done | bytes 1048592 | tf_op jit(solution)/shard_map/all_gather | solution.py:72
  149.6 1.9 convolution_convert_fusion.1
  151.7 2.1 convert_bitcast_fusion.1
  153.8 5.0 %fusion.32 = f32[4,128,128]{2,1,0:T(8,128)} fusion(bf16[4,16,128,128]{3,2,1,0:T(8,128)(2,1)S(1)} %copy-done, bf16[4,16,128,128]{3,2,1,0:T(8,128)(2,1)} %param.6, bf16[4,16,128,128]{3,1,2,0:T(8,128)(2,1)} %convert_bitcast_fusion.1), kind=kOutput, calls=%fused_computation.23 | convolution fusion | flops 537919488 | bytes 6553600 | tf_op jit(solution)/shard_map/pwik,pwkl->pil/dot_general | solution.py:46
  158.9 35.4 %all-reduce.6.cloned.1.call-done = f32[4,128,128]{2,1,0:T(8,128)} async-done(((f32[4,128,128]{2,1,0:T(8,128)}), f32[4,128,128]{2,1,0:T(8,128)}) %all-reduce.6.cloned.1.call-update) | async-done | bytes 262160 | tf_op jit(solution)/shard_map/psum | solution.py:77
  194.3 1.7 multiply_reduce_fusion.3
  196.0 12.8 %psum.75 = f32[]{:T(128)} all-reduce(f32[]{:T(128)} %multiply_reduce_fusion.3), channel_id=1, replica_groups=mesh['sector'=8,'op'=4] {'sector'}, use_global_device_ids=true, to_apply=%region_10.11 | all-reduce | flops 1 | bytes 8 | tf_op jit(solution)/shard_map/psum | solution.py:78
  209.5 1.7 multiply_reduce_fusion.2
  211.2 12.4 %psum.76 = f32[]{:T(128)} all-reduce(f32[]{:T(128)} %get-tuple-element.7), channel_id=1, replica_groups=mesh['sector'=8,'op'=4] {'sector'}, use_global_device_ids=true, to_apply=%region_12.13 | all-reduce | flops 1 | bytes 8 | tf_op jit(solution)/shard_map/psum | solution.py:60
  225.2 21.9 %all-gather.8.cloned.1.call-done = bf16[32,128,128]{2,1,0:T(8,128)(2,1)} async-done(((bf16[4,128,128]{2,1,0:T(8,128)(2,1)}), bf16[32,128,128]{2,1,0:T(8,128)(2,1)}) %all-gather.8.cloned.1.call-update) | async-done | bytes 1048592 | tf_op jit(solution)/shard_map/all_gather | solution.py:72
  247.1 1.9 convolution_convert_fusion
  249.1 2.1 convert_bitcast_fusion
  251.2 5.0 %fusion.37 = f32[4,128,128]{2,1,0:T(8,128)} fusion(bf16[4,16,128,128]{3,2,1,0:T(8,128)(2,1)S(1)} %copy-done, bf16[4,16,128,128]{3,2,1,0:T(8,128)(2,1)} %param.6, bf16[4,16,128,128]{3,1,2,0:T(8,128)(2,1)} %convert_bitcast_fusion), kind=kOutput, calls=%fused_computation.24 | convolution fusion | flops 537919488 | bytes 6553600 | tf_op jit(solution)/shard_map/pwik,pwkl->pil/dot_general | solution.py:46
  256.3 35.5 %all-reduce.8.cloned.1.call-done = f32[4,128,128]{2,1,0:T(8,128)} async-done(((f32[4,128,128]{2,1,0:T(8,128)}), f32[4,128,128]{2,1,0:T(8,128)}) %all-reduce.8.cloned.1.call-update) | async-done | bytes 262160 | tf_op jit(solution)/shard_map/psum | solution.py:77
  291.7 1.7 multiply_reduce_fusion.1
  293.4 12.8 %psum.78 = f32[]{:T(128)} all-reduce(f32[]{:T(128)} %multiply_reduce_fusion.1), channel_id=1, replica_groups=mesh['sector'=8,'op'=4] {'sector'}, use_global_device_ids=true, to_apply=%region_15.16 | all-reduce | flops 1 | bytes 8 | tf_op jit(solution)/shard_map/psum | solution.py:78
  306.9 1.7 multiply_reduce_fusion
  308.6 12.4 %psum.79 = f32[]{:T(128)} all-reduce(f32[]{:T(128)} %get-tuple-element.5), channel_id=1, replica_groups=mesh['sector'=8,'op'=4] {'sector'}, use_global_device_ids=true, to_apply=%region_17.18 | all-reduce | flops 1 | bytes 8 | tf_op jit(solution)/shard_map/psum | solution.py:60
  (38 shorter events, 6.1 us)
Async XLA Ops:
  7.2 48.0 %copy-start = (bf16[4,16,128,128]{3,2,1,0:T(8,128)(2,1)S(1)}, bf16[4,16,128,128]{3,2,1,0:T(8,128)(2,1)}, u32[]{:S(2)}) copy-start(bf16[4,16,128,128]{3,2,1,0:T(8,128)(2,1)} %param.7) | copy-start | bytes 6291460
  7.2 43.9 %all-gather.4.cloned.1.call-start = ((), (), s32[]{:S(2)}) async-start(), calls=%async_computation | async-start | bytes 1179648 | tf_op jit(solution)/shard_map/all_gather | solution.py:72
  28.0 67.7 %all-reduce.4.cloned.1.call-start = ((), (), s32[]{:S(2)}) async-start(), calls=%async_computation.1 | async-start | bytes 524288 | tf_op jit(solution)/shard_map/psum | solution.py:77
  55.2 40.6 %copy-start.1 = (f32[4,128,128]{2,1,0:T(8,128)S(1)}, f32[4,128,128]{2,1,0:T(8,128)}, u32[]{:S(2)}) copy-start(f32[4,128,128]{2,1,0:T(8,128)} %param.5) | copy-start | bytes 786436
  60.3 89.4 %all-gather.6.cloned.1.call-start = ((), (), s32[]{:S(2)}) async-start(), calls=%async_computation.2 | async-start | bytes 1179648 | tf_op jit(solution)/shard_map/all_gather | solution.py:72
  127.6 66.7 %all-reduce.6.cloned.1.call-start = ((), (), s32[]{:S(2)}) async-start(), calls=%async_computation.3 | async-start | bytes 524288 | tf_op jit(solution)/shard_map/psum | solution.py:77
  158.8 88.3 %all-gather.8.cloned.1.call-start = ((), (), s32[]{:S(2)}) async-start(), calls=%async_computation.4 | async-start | bytes 1179648 | tf_op jit(solution)/shard_map/all_gather | solution.py:72
  225.0 66.7 %all-reduce.8.cloned.1.call-start = ((), (), s32[]{:S(2)}) async-start(), calls=%async_computation.5 | async-start | bytes 524288 | tf_op jit(solution)/shard_map/psum | solution.py:77
  321.7 2.0 copy-start.2
Sparse Core Ops, SparseCore 0:
  28.2 22.8 all-gather.3
  60.4 35.3 all-reduce.3
  127.7 21.9 all-gather.5
  158.9 35.2 all-reduce.5
  225.1 21.9 all-gather.7
  256.4 35.2 all-reduce.7
where the time goes:
time: 331 us
  waiting for transfers between devices  169 us (51%)
  blocking collectives  91.5 us (28%)
  matrix products  28.4 us (9%)
  between operations  19 us (6%)
  other arithmetic  18.5 us (6%)
  local copies, waits for them, and re-layouts  3.32 us (1%)
    psum x3, waiting for transfers between devices, per_device(): image = lax.psum(partial_sum, 'op') * scale * mask  106 us
    all_gather x3, waiting for transfers between devices, per_device(): lax.all_gather(vector.astype(jnp.bfloat16), 'sector', axis=0, tiled=True)  63 us
    psum x4, blocking collectives, sq_sum(): return lax.psum(jnp.sum(first * first), 'sector')  53 us
    psum x3, blocking collectives, per_device(): alpha = lax.psum(jnp.sum(vector * image), 'sector') / count  38.5 us
    dot_general x3, matrix products, term_products(): jnp.einsum('pwik,pwkl->pil', inner, right_env, preferred_element_type=jnp...  15 us
    reduce_sum x4, other arithmetic, sq_sum(): return lax.psum(jnp.sum(first * first), 'sector')  6.82 us
  transfers between devices with their start and end apart: 6, of which 6 were waited for; matrix products, arithmetic and copies ran while one was open for 1% of the time, Pallas kernels for 0%

commit v1 on v0

v1 whole, which is shorter than its diff:
```python
import functools

import jax
import jax.numpy as jnp
from jax import lax
from jax.experimental import pallas as pl
from jax.experimental.pallas import tpu as pltpu
from jax.sharding import PartitionSpec as P

MESH = pl.DeviceIdType.MESH
F32 = jnp.float32
BF16 = jnp.bfloat16
STEPS = 3


def kernel(
    n_sec, n_op,
    theta_ref, left_hbm, right_hbm, perm_ref, dims_ref,
    vec_ref, coef_ref, dens_ref,
    left_v, right_v, gath, pb, rsb, az, ap,
    env_sem, rsem, zsend, psend, fsend, rs_send, rs_recv,
    az_send, az_recv, ap_send, ap_recv,
):
    sec_dev, width, _ = theta_ref.shape
    term_dev = left_hbm.shape[1]
    total = n_sec * sec_dev
    count = float(total * width * width)
    scale = float((term_dev * n_op) ** -0.5)
    rows = sec_dev * width // n_op
    cpb = width // rows
    n_chip = n_sec // 2
    aligned = n_op == sec_dev

    s = lax.axis_index("sector")
    z = lax.axis_index("op")
    core = lax.rem(s, 2)
    chip = s // 2
    sib = s + 1 - 2 * core
    peers = [2 * lax.rem(chip + m, n_chip) + core for m in range(1, n_chip)]
    others = [2 * lax.rem(chip + m, n_chip) + 1 - core for m in range(n_chip)]
    mates = [lax.rem(z + m, n_op) for m in range(1, n_op)]
    plane = [lax.rem(s + m, n_sec) for m in range(1, n_sec)]

    env = []
    for p in range(sec_dev):
        env.append(pltpu.make_async_copy(left_hbm.at[p], left_v.at[p], env_sem.at[0, p]))
        env.append(pltpu.make_async_copy(right_hbm.at[p], right_v.at[p], env_sem.at[1, p]))
    for copy in env:
        copy.start()

    barrier = pltpu.get_barrier_semaphore()
    for other in plane:
        pl.semaphore_signal(barrier, inc=1, device_id=(other, z), device_id_type=MESH)
    for other in mates:
        pl.semaphore_signal(barrier, inc=1, device_id=(s, other), device_id_type=MESH)

    def block_mask(p, first, n):
        r = lax.broadcasted_iota(jnp.int32, (n, width), 0) + first
        c = lax.broadcasted_iota(jnp.int32, (n, width), 1)
        return jnp.where((r < dims_ref[p, 0]) & (c < dims_ref[p, 1]), 1.0, 0.0).astype(F32)

    def chunk(ref, base, j):
        if cpb == 1:
            return ref.at[base + j]
        return ref.at[base + j // cpb, pl.ds(pl.multiple_of(lax.rem(j, cpb) * rows, rows), rows)]

    def slot(owner, j):
        return chunk(gath, owner * sec_dev, j)

    def row(owner):
        return gath.at[pl.ds(owner * sec_dev, sec_dev)]

    def send(src, dst, ssem, dsem, dev):
        copy = pltpu.make_async_remote_copy(
            src_ref=src, dst_ref=dst, send_sem=ssem, recv_sem=dsem,
            device_id=dev, device_id_type=MESH,
        )
        copy.start()
        return copy

    def arrived(dst, dsem):
        pltpu.make_async_remote_copy(
            src_ref=dst, dst_ref=dst, send_sem=zsend.at[0], recv_sem=dsem,
            device_id=(sib, z), device_id_type=MESH,
        ).wait_recv()

    def fold(x):
        return jnp.sum(x.reshape(x.shape[0] // 8, 8, width), axis=0)

    def whole(x):
        return jnp.sum(x, keepdims=True)

    own_p = z // cpb
    own_r = pl.multiple_of(lax.rem(z, cpb) * rows, rows)
    mask = block_mask(own_p, own_r, rows)
    for p in range(sec_dev):
        gath[s * sec_dev + p] = (theta_ref[p] * block_mask(p, 0, width)).astype(BF16)
    u = theta_ref[own_p, pl.ds(own_r, rows), :] * mask
    rr = fold(u * u)

    pl.semaphore_wait(barrier, n_sec - 1 + n_op - 1)

    sends = []
    for i, peer in enumerate(peers + [sib]):
        sends.append(send(row(s), row(s), psend.at[0, i], rsem.at[s, 0], (peer, z)))

    order = [lax.rem(z + 1 + i, sec_dev) if aligned else i for i in range(sec_dev)]
    wants = []
    for p in order:
        mine = perm_ref[s * sec_dev + p]
        for c in range(3):
            q = lax.rem(z * term_dev + c, 3)
            wants.append(lax.rem(mine + q - 1 + total, total))

    def look(i, found):
        here = perm_ref[i]
        return tuple(jnp.where(here == w, i, f) for w, f in zip(wants, found))

    src = lax.fori_loop(0, total, look, tuple(jnp.int32(0) for _ in wants))

    for i, peer in enumerate(peers):
        arrived(row(peer), rsem.at[peer, 0])
        sends.append(send(row(peer), row(peer), fsend.at[0, i], rsem.at[peer, 0], (sib, z)))
    for other in others:
        arrived(row(other), rsem.at[other, 0])
    for copy in env:
        copy.wait()

    def reduce_scalars(use, tiles):
        az[use, z] = tiles
        out = []
        for i, mate in enumerate(mates):
            out.append(send(az.at[use, z], az.at[use, z], az_send.at[use, i], az_recv.at[use, z], (s, mate)))
        for mate in mates:
            arrived(az.at[use, mate], az_recv.at[use, mate])
        acc = az[use, 0]
        for j in range(1, n_op):
            acc = acc + az[use, j]
        ap[use, s] = acc
        for i, other in enumerate(plane):
            out.append(send(ap.at[use, s], ap.at[use, s], ap_send.at[use, i], ap_recv.at[use, s], (other, z)))
        for other in plane:
            arrived(ap.at[use, other], ap_recv.at[use, other])
        acc = ap[use, 0]
        for j in range(1, n_sec):
            acc = acc + ap[use, j]
        for copy in out:
            copy.wait_send()
        return whole(acc[0:8]), whole(acc[8:16])

    prev = jnp.zeros_like(u)
    alphas, betas = [], []
    for step in range(STEPS):
        if step > 0:
            slot(s, z)[...] = u.astype(BF16)
            sends = []
            for i, mate in enumerate(mates):
                sends.append(send(slot(s, z), slot(s, z), zsend.at[i], rsem.at[s, z], (s, mate)))
            for m, j in enumerate([z] + mates):
                if m > 0:
                    arrived(slot(s, j), rsem.at[s, j])
                for i, peer in enumerate(peers + [sib]):
                    sends.append(send(slot(s, j), slot(s, j), psend.at[m, i], rsem.at[s, j], (peer, z)))
            for m, j in enumerate([z] + mates):
                for i, peer in enumerate(peers):
                    arrived(slot(peer, j), rsem.at[peer, j])
                    sends.append(send(slot(peer, j), slot(peer, j), fsend.at[m, i], rsem.at[peer, j], (sib, z)))
            for j in [z] + mates:
                for other in others:
                    arrived(slot(other, j), rsem.at[other, j])

        dot_acc = jnp.zeros((8, width), F32)
        rs = []
        for i, p in enumerate(order):
            inner = [None] * term_dev
            for c in range(3):
                terms = list(range(c, term_dev, 3))
                lhs = jnp.concatenate([left_v[p, t] for t in terms], axis=0)
                got = jnp.dot(lhs, gath[src[3 * i + c]], preferred_element_type=F32).astype(BF16)
                for n, t in enumerate(terms):
                    inner[t] = got[n * width:(n + 1) * width]
            part = jnp.dot(
                jnp.concatenate(inner, axis=1),
                right_v[p].reshape(term_dev * width, width),
                preferred_element_type=F32,
            )
            pb[p] = part.astype(BF16)
            dot_acc = dot_acc + fold(part * gath[s * sec_dev + p].astype(F32))
            if aligned and i < sec_dev - 1:
                rs.append(send(pb.at[p], rsb.at[z], rs_send.at[i], rs_recv.at[z], (s, p)))
        if not aligned:
            for i, mate in enumerate(mates):
                rs.append(send(chunk(pb, 0, mate), rsb.at[z], rs_send.at[i], rs_recv.at[z], (s, mate)))
        rsb[z] = chunk(pb, 0, z)[...]
        for copy in sends:
            copy.wait_send()

        a_sum, n_sum = reduce_scalars(step % 2, jnp.concatenate([dot_acc, rr], axis=0))
        norm = jnp.sqrt(n_sum / count + 1e-06)
        inv = 1.0 / norm
        alpha = a_sum * (scale / count) * inv * inv
        alphas.append(alpha)
        if step > 0:
            betas.append(norm)

        for mate in mates:
            arrived(rsb.at[mate], rs_recv.at[mate])
        image = rsb[0].astype(F32)
        for j in range(1, n_op):
            image = image + rsb[j].astype(F32)
        for copy in rs:
            copy.wait_send()
        v = u * inv
        resid = image * mask * (inv * scale) - alpha * v
        if step > 0:
            resid = resid - norm * prev
        prev, u = v, resid
        rr = fold(u * u)

    slot(s, z)[...] = u.astype(BF16)
    sends = []
    for i, mate in enumerate(mates):
        sends.append(send(slot(s, z), slot(s, z), zsend.at[i], rsem.at[s, z], (s, mate)))
    _, n_sum = reduce_scalars(STEPS % 2, jnp.concatenate([rr, rr], axis=0))
    norm = jnp.sqrt(n_sum / count + 1e-06)
    inv = 1.0 / norm
    betas.append(norm)
    lane = lax.broadcasted_iota(jnp.int32, (8, 128), 1)
    coef = jnp.zeros((8, 128), F32)
    for i, value in enumerate(alphas + betas):
        coef = jnp.where(lane == i, value, coef)
    coef_ref[...] = coef
    for mate in mates:
        arrived(slot(s, mate), rsem.at[s, mate])
    for p in range(sec_dev):
        block = gath[s * sec_dev + p]
        vec_ref[p] = block.astype(F32) * inv
        outer = lax.dot_general(block, block, (((1,), (1,)), ((), ())), preferred_element_type=F32)
        dens_ref[p] = outer * (inv * inv * (1.0 / width))
    for copy in sends:
        copy.wait_send()


def per_device(theta, left_env, right_env, perm, dims):
    sec_dev, width, _ = theta.shape
    term_dev = left_env.shape[1]
    n_sec, n_op = lax.axis_size("sector"), lax.axis_size("op")
    rows = sec_dev * width // n_op
    n_chip = n_sec // 2
    dma = pltpu.SemaphoreType.DMA
    vmem = pl.BlockSpec(memory_space=pltpu.VMEM)
    smem = pl.BlockSpec(memory_space=pltpu.SMEM)
    hbm = pl.BlockSpec(memory_space=pl.ANY)
    vec, coef, dens = pl.pallas_call(
        functools.partial(kernel, n_sec, n_op),
        out_shape=(
            jax.ShapeDtypeStruct(theta.shape, F32),
            jax.ShapeDtypeStruct((8, 128), F32),
            jax.ShapeDtypeStruct(theta.shape, F32),
        ),
        in_specs=[vmem, hbm, hbm, smem, smem],
        out_specs=(vmem, vmem, vmem),
        scratch_shapes=[
            pltpu.VMEM(left_env.shape, BF16),
            pltpu.VMEM(right_env.shape, BF16),
            pltpu.VMEM((n_sec * sec_dev, width, width), BF16),
            pltpu.VMEM((sec_dev, width, width), BF16),
            pltpu.VMEM((n_op, rows, width), BF16),
            pltpu.VMEM((2, n_op, 16, width), F32),
            pltpu.VMEM((2, n_sec, 16, width), F32),
            dma((2, sec_dev)),
            dma((n_sec, n_op)),
            dma((n_op,)),
            dma((n_op, n_chip)),
            dma((n_op, n_chip)),
            dma((n_op,)),
            dma((n_op,)),
            dma((2, n_op)),
            dma((2, n_op)),
            dma((2, n_sec)),
            dma((2, n_sec)),
        ],
        compiler_params=pltpu.CompilerParams(
            collective_id=0, has_side_effects=True, vmem_limit_bytes=40 * 1024 * 1024
        ),
        cost_estimate=pl.CostEstimate(
            flops=STEPS * 4 * sec_dev * term_dev * width**3,
            bytes_accessed=4 * sec_dev * term_dev * width**2,
            transcendentals=0,
        ),
    )(theta, left_env, right_env, perm, dims)
    return vec, coef[0, :6], dens


def solution(mesh):
    placed = (
        P("sector", None, None),
        P("sector", "op", None, None),
        P("sector", "op", None, None),
        P(),
        P("sector", None),
    )
    return jax.shard_map(
        per_device,
        mesh=mesh,
        in_specs=placed,
        out_specs=(P("sector", None, None), P(), P("sector", None, None)),
        check_vma=False,
    )
```

time: 331 us -> 83.4 us (0.25)
  waiting for transfers between devices: 169 us -> 0 us
  blocking collectives: 91.5 us -> 0 us
  Pallas kernels: 0 us -> 75 us
  matrix products: 28.4 us -> 0 us
  other arithmetic: 18.5 us -> 0 us
  between operations: 19 us -> 0.64 us
  local copies, waits for them, and re-layouts: 3.32 us -> 7.47 us
    psum x3 -> x0, waiting for transfers between devices: 106 us -> none  [per_device(): image = lax.psum(partial_sum, 'op') * scale * mask]
    psum x7 -> x0, blocking collectives: 91.5 us -> none  [the longest x4 53 us: sq_sum(): return lax.psum(jnp.sum(first * first), 'sector')]
    pallas_call x0 -> x1, Pallas kernels: none -> 75 us  [per_device(): pl.pallas_call(functools.partial(kernel, n_sec, n_op), out_shape=(jax.Sha...]
    all_gather x3 -> x0, waiting for transfers between devices: 63 us -> none  [per_device(): lax.all_gather(vector.astype(jnp.bfloat16), 'sector', axis=0, tiled=True)]
    dot_general x10 -> x0, matrix products: 28.4 us -> none  [the longest x3 15 us: term_products(): jnp.einsum('pwik,pwkl->pil', inner, right_env, preferred_element_type=jnp...]
    reduce_sum x7 -> x0, other arithmetic: 11.9 us -> none  [the longest x4 6.82 us: sq_sum(): return lax.psum(jnp.sum(first * first), 'sector')]
    unnamed x12 -> x11, local copies, waits for them, and re-layouts: 0.4 us -> 6.96 us
    convert_element_type x4 -> x0, other arithmetic: 4.26 us -> none  [the longest x3 4.18 us: per_device(): vector.astype(jnp.bfloat16)]
  transfers between devices with their start and end apart: 6 -> 0, of which waited for: 6 -> 0; matrix products, arithmetic and copies ran while one was open for 1% -> 0% of each run, Pallas kernels for 0% -> 0%
where the time goes in v1:
time: 83.4 us; the launch traced here: 83.1 us
  Pallas kernels  75 us (90%)
  local copies, waits for them, and re-layouts  7.47 us (9%)
    pallas_call x1, Pallas kernels, per_device(): pl.pallas_call(functools.partial(kernel, n_sec, n_op), out_shape=(jax.Sha...  75 us
    unnamed x11, local copies, waits for them, and re-layouts  6.96 us

profile of v1, /device:TPU:0, one launch (start us, length us, event | category | flops | bytes accessed | tf_op | source)
XLA Modules:
  0.0 83.1 jit_solution(3851703036996912676)
XLA Ops:
  0.6 0.8 copy.8.dims_ref
  1.4 0.0 copy-start
  1.4 1.6 %copy-done = bf16[4,16,128,128]{3,2,1,0:T(8,128)(2,1)S(1)} copy-done((bf16[4,16,128,128]{3,2,1,0:T(8,128)(2,1)S(1)}, bf16[4,16,128,128]{3,2,1,0:T(8,128)(2,1)}, u32[]{:S(2)}) %copy-start) | copy-done | bytes 2097176
  3.0 0.0 copy-start.1
  3.0 1.6 %copy-done.1 = bf16[4,16,128,128]{3,2,1,0:T(8,128)(2,1)S(1)} copy-done((bf16[4,16,128,128]{3,2,1,0:T(8,128)(2,1)S(1)}, bf16[4,16,128,128]{3,2,1,0:T(8,128)(2,1)}, u32[]{:S(2)}) %copy-start.1) | copy-done | bytes 2097176
  4.6 0.0 copy-start.2
  4.6 0.9 %copy-done.2 = f32[4,128,128]{2,1,0:T(8,128)S(1)} copy-done((f32[4,128,128]{2,1,0:T(8,128)S(1)}, f32[4,128,128]{2,1,0:T(8,128)}, u32[]{:S(2)}) %copy-start.2) | copy-done | bytes 262168
  5.5 0.0 copy-start.3
  5.5 0.7 copy-done.3
  6.2 75.0 %shard_map.76 = (f32[4,128,128]{2,1,0:T(8,128)S(1)}, f32[8,128]{1,0:T(8,128)S(1)}, f32[4,128,128]{2,1,0:T(8,128)S(1)}) custom-call(f32[4,128,128]{2,1,0:T(8,128)S(1)} %copy-done.2, bf16[4,16,128,128]{3,2,1,0:T(8,128)(2,1)S(1)} %copy-done, bf16[4,16,128,128]{3,2,1,0:T(8,128)(2,1)S(1)} %copy-done.1, s32[32]{0:T(128)S(1)} %copy-done.3, s32[4,2]{1,0:T(4,128)S(1)} %copy.8.dims_ref), custom_call_target="tpu_custom_call" | custom-call | flops 1610612736 | bytes 4194304 | tf_op jit(solution)/shard_map/pallas_call | solution.py:254
  81.2 0.5 slice_bitcast_fusion
  81.7 0.7 copy.11
  82.4 0.7 copy.12
Async XLA Ops:
  1.4 1.6 %copy-start = (bf16[4,16,128,128]{3,2,1,0:T(8,128)(2,1)S(1)}, bf16[4,16,128,128]{3,2,1,0:T(8,128)(2,1)}, u32[]{:S(2)}) copy-start(bf16[4,16,128,128]{3,2,1,0:T(8,128)(2,1)} %left_hbm.1) | copy-start | bytes 6291460
  3.0 1.6 %copy-start.1 = (bf16[4,16,128,128]{3,2,1,0:T(8,128)(2,1)S(1)}, bf16[4,16,128,128]{3,2,1,0:T(8,128)(2,1)}, u32[]{:S(2)}) copy-start(bf16[4,16,128,128]{3,2,1,0:T(8,128)(2,1)} %right_hbm.1) | copy-start | bytes 6291460
  4.6 0.9 %copy-start.2 = (f32[4,128,128]{2,1,0:T(8,128)S(1)}, f32[4,128,128]{2,1,0:T(8,128)}, u32[]{:S(2)}) copy-start(f32[4,128,128]{2,1,0:T(8,128)} %theta_ref.1) | copy-start | bytes 786436
  5.5 0.7 copy-start.3

commit v2 on v1

v2 whole, which is shorter than its diff:
```python
import functools

import jax
import jax.numpy as jnp
from jax import lax
from jax.experimental import pallas as pl
from jax.experimental.pallas import tpu as pltpu
from jax.sharding import PartitionSpec as P

MESH = pl.DeviceIdType.MESH
F32 = jnp.float32
BF16 = jnp.bfloat16
STEPS = 3


def kernel(
    n_sec, n_op,
    theta_hbm, left_hbm, right_hbm, perm_ref, dims_ref,
    vec_ref, coef_ref, dens_ref,
    theta_v, left_v, right_v, gath_a, gath_b, basis, pb, rsb, az, ap,
    env_sem, rsem, zsend, psend, fsend, relay, rs_send, rs_recv,
    az_send, az_recv, ap_send, ap_recv,
):
    gath = (gath_a, gath_b)
    sec_dev, width, _ = theta_v.shape
    term_dev = left_v.shape[1]
    total = n_sec * sec_dev
    count = float(total * width * width)
    scale = float((term_dev * n_op) ** -0.5)
    rows = sec_dev * width // n_op
    cpb = width // rows
    n_chip = n_sec // 2
    aligned = n_op == sec_dev
    square = n_chip == 4

    s = lax.axis_index("sector")
    z = lax.axis_index("op")
    core = lax.rem(s, 2)
    chip = s // 2
    sib = s + 1 - 2 * core
    if square:
        beside = [chip + 1 - 2 * lax.rem(chip, 2), lax.rem(chip + 2, 4), 3 - chip]
    else:
        beside = [lax.rem(chip + m, n_chip) for m in range(1, n_chip)]
    peers = [2 * c + core for c in beside]
    direct = peers[:2] if square else peers
    others = [sib] + [2 * c + 1 - core for c in beside]
    mates = [lax.rem(z + m, n_op) for m in range(1, n_op)]
    plane = [lax.rem(s + m, n_sec) for m in range(1, n_sec)]

    fetch = pltpu.make_async_copy(theta_hbm, theta_v, env_sem.at[2, 0])
    fetch.start()
    env = []
    for p in range(sec_dev):
        env.append(pltpu.make_async_copy(left_hbm.at[p], left_v.at[p], env_sem.at[0, p]))
        env.append(pltpu.make_async_copy(right_hbm.at[p], right_v.at[p], env_sem.at[1, p]))
    for copy in env:
        copy.start()

    barrier = pltpu.get_barrier_semaphore()
    for other in plane:
        pl.semaphore_signal(barrier, inc=1, device_id=(other, z), device_id_type=MESH)
    for other in mates:
        pl.semaphore_signal(barrier, inc=1, device_id=(s, other), device_id_type=MESH)

    def block_mask(p, first, n):
        r = lax.broadcasted_iota(jnp.int32, (n, width), 0) + first
        c = lax.broadcasted_iota(jnp.int32, (n, width), 1)
        return jnp.where((r < dims_ref[p, 0]) & (c < dims_ref[p, 1]), 1.0, 0.0).astype(F32)

    def chunk(ref, base, j):
        if cpb == 1:
            return ref.at[base + j]
        return ref.at[base + j // cpb, pl.ds(pl.multiple_of(lax.rem(j, cpb) * rows, rows), rows)]

    def slot(g, owner, j):
        return chunk(gath[g], owner * sec_dev, j)

    def send(src, dst, ssem, dsem, dev):
        copy = pltpu.make_async_remote_copy(
            src_ref=src, dst_ref=dst, send_sem=ssem, recv_sem=dsem,
            device_id=dev, device_id_type=MESH,
        )
        copy.start()
        return copy

    def arrived(dst, dsem):
        pltpu.make_async_remote_copy(
            src_ref=dst, dst_ref=dst, send_sem=zsend.at[0], recv_sem=dsem,
            device_id=(sib, z), device_id_type=MESH,
        ).wait_recv()

    def fold(x):
        return jnp.sum(x.reshape(x.shape[0] // 8, 8, width), axis=0)

    def whole(x):
        return jnp.sum(x, keepdims=True)

    def move(g, j, owner, ssem, dev):
        return send(slot(g, owner, j), slot(g, owner, j), ssem, rsem.at[g, owner, j], (dev, z))

    def spread_z(g):
        return [
            send(slot(g, s, z), slot(g, s, z), zsend.at[i], rsem.at[g, s, z], (s, mate))
            for i, mate in enumerate(mates)
        ]

    def spread_plane(g, m, j):
        return [move(g, j, s, psend.at[m, i], dev) for i, dev in enumerate(direct + [sib])]

    def pass_on(g, m, j):
        out = []
        for i, peer in enumerate(peers):
            arrived(slot(g, peer, j), rsem.at[g, peer, j])
            if square and i == m % 2:
                out.append(move(g, j, peer, relay.at[m], peers[1 - i]))
            out.append(move(g, j, peer, fsend.at[m, i], sib))
        return out

    def collect(g):
        for j in [z] + mates:
            for other in others:
                arrived(slot(g, other, j), rsem.at[g, other, j])

    own_p = z // cpb
    own_r = pl.multiple_of(lax.rem(z, cpb) * rows, rows)
    mask = block_mask(own_p, own_r, rows)
    fetch.wait()
    for p in range(sec_dev):
        gath[0][s * sec_dev + p] = (theta_v[p] * block_mask(p, 0, width)).astype(BF16)

    pl.semaphore_wait(barrier, n_sec - 1 + n_op - 1)

    sends = []
    for m, j in enumerate([z] + mates):
        sends += spread_plane(0, m, j)

    order = [lax.rem(z + 1 + i, sec_dev) if aligned else i for i in range(sec_dev)]
    wants = []
    for p in order:
        mine = perm_ref[s * sec_dev + p]
        for c in range(3):
            q = lax.rem(z * term_dev + c, 3)
            wants.append(lax.rem(mine + q - 1 + total, total))
    own_c = lax.rem(3 * term_dev * n_op + 1 - z * term_dev, 3)

    def look(i, found):
        here = perm_ref[i]
        return tuple(jnp.where(here == w, i, f) for w, f in zip(wants, found))

    src = lax.fori_loop(0, total, look, tuple(jnp.int32(0) for _ in wants))

    for m, j in enumerate([z] + mates):
        sends += pass_on(0, m, j)
    collect(0)
    for copy in env:
        copy.wait()

    def share(use):
        return [
            send(az.at[use, z], az.at[use, z], az_send.at[use, i], az_recv.at[use, z], (s, mate))
            for i, mate in enumerate(mates)
        ]

    def add_op(use):
        for mate in mates:
            arrived(az.at[use, mate], az_recv.at[use, mate])
        acc = az[use, 0]
        for j in range(1, n_op):
            acc = acc + az[use, j]
        return acc

    def share_plane(use, tiles):
        ap[use, s] = tiles
        return [
            send(ap.at[use, s], ap.at[use, s], ap_send.at[use, i], ap_recv.at[use, s], (other, z))
            for i, other in enumerate(plane)
        ]

    def add_plane(use):
        for other in plane:
            arrived(ap.at[use, other], ap_recv.at[use, other])
        acc = ap[use, 0]
        for j in range(1, n_sec):
            acc = acc + ap[use, j]
        return whole(acc[0:8]), whole(acc[8:16])

    def recur(k, block, where):
        value = block * weights[0] + basis[k - 1, where] * weights[1]
        if k > 1:
            value = value + basis[k - 2, where] * weights[2]
        return value

    weights = None
    last_inv = None
    alphas, betas = [], []
    for step in range(STEPS):
        g, nxt, use = step % 2, (step + 1) % 2, step % 2

        dot_acc = jnp.zeros((8, width), F32)
        rr = jnp.zeros((8, width), F32)
        rs = []
        for i, p in enumerate(order):
            inner = [None] * term_dev
            for c in range(3):
                x = gath[g][src[3 * i + c]].astype(F32)
                if step > 0:
                    x = recur(step, x, 3 * i + c)
                basis[step, 3 * i + c] = x
                terms = list(range(c, term_dev, 3))
                lhs = jnp.concatenate([left_v[p, t] for t in terms], axis=0)
                got = jnp.dot(lhs, x.astype(BF16), preferred_element_type=F32).astype(BF16)
                for n, t in enumerate(terms):
                    inner[t] = got[n * width:(n + 1) * width]
            part = jnp.dot(
                jnp.concatenate(inner, axis=1),
                right_v[p].reshape(term_dev * width, width),
                preferred_element_type=F32,
            )
            pb[p] = part.astype(BF16)
            dot_acc = dot_acc + fold(part * basis[step, 3 * i + own_c])
            if aligned and i < sec_dev - 1:
                rs.append(send(pb.at[p], rsb.at[z], rs_send.at[i], rs_recv.at[z], (s, p)))
        if not aligned:
            for i, mate in enumerate(mates):
                rs.append(send(chunk(pb, 0, mate), rsb.at[z], rs_send.at[i], rs_recv.at[z], (s, mate)))
        for p in range(sec_dev):
            i = lax.rem(p + 2 * sec_dev - 1 - z, sec_dev) if aligned else p
            own = basis[step, 3 * i + own_c]
            rr = rr + fold(own * own)
        az[use, z] = dot_acc
        small = share(use)
        rsb[z] = chunk(pb, 0, z)[...]
        for copy in sends:
            copy.wait_send()
        for mate in mates:
            arrived(rsb.at[mate], rs_recv.at[mate])
        image = rsb[0].astype(F32)
        for j in range(1, n_op):
            image = image + rsb[j].astype(F32)
        slot(nxt, s, z)[...] = (image * mask).astype(BF16)
        sends = spread_z(nxt)
        last = step == STEPS - 1
        if not last:
            sends += spread_plane(nxt, 0, z)
        small += share_plane(use, jnp.concatenate([add_op(use), rr], axis=0))
        if not last:
            for m, j in enumerate(mates):
                arrived(slot(nxt, s, j), rsem.at[nxt, s, j])
                sends += spread_plane(nxt, m + 1, j)
            sends += pass_on(nxt, 0, z)
        a_sum, n_sum = add_plane(use)
        norm = jnp.sqrt(n_sum / count + 1e-06)
        inv = 1.0 / norm
        alpha = a_sum * (scale / count) * inv * inv
        weights = [inv * scale, -alpha * inv]
        if step > 0:
            weights.append(-norm * last_inv)
            betas.append(norm)
        last_inv = inv
        alphas.append(alpha)
        if not last:
            for m, j in enumerate(mates):
                sends += pass_on(nxt, m + 1, j)
        for copy in rs + small:
            copy.wait_send()
        if not last:
            collect(nxt)

    g, use = STEPS % 2, STEPS % 2
    for mate in mates:
        arrived(slot(g, s, mate), rsem.at[g, s, mate])
    rr = jnp.zeros((8, width), F32)
    for i, p in enumerate(order):
        u = recur(STEPS, gath[g][s * sec_dev + p].astype(F32), 3 * i + own_c)
        theta_v[p] = u
        pb[p] = u.astype(BF16)
    for p in range(sec_dev):
        rr = rr + fold(theta_v[p] * theta_v[p])
    small = share_plane(use, jnp.concatenate([rr, rr], axis=0))
    for p in range(sec_dev):
        block = pb[p]
        dens_ref[p] = lax.dot_general(block, block, (((1,), (1,)), ((), ())), preferred_element_type=F32)
    _, n_sum = add_plane(use)
    norm = jnp.sqrt(n_sum / count + 1e-06)
    inv = 1.0 / norm
    betas.append(norm)
    for p in range(sec_dev):
        vec_ref[p] = theta_v[p] * inv
        dens_ref[p] = dens_ref[p] * (inv * inv * (1.0 / width))
    lane = lax.broadcasted_iota(jnp.int32, (8, 128), 1)
    coef = jnp.zeros((8, 128), F32)
    for i, value in enumerate(alphas + betas):
        coef = jnp.where(lane == i, value, coef)
    coef_ref[...] = coef
    for copy in sends + small:
        copy.wait_send()


def per_device(theta, left_env, right_env, perm, dims):
    sec_dev, width, _ = theta.shape
    term_dev = left_env.shape[1]
    n_sec, n_op = lax.axis_size("sector"), lax.axis_size("op")
    rows = sec_dev * width // n_op
    n_chip = n_sec // 2
    dma = pltpu.SemaphoreType.DMA
    vmem = pl.BlockSpec(memory_space=pltpu.VMEM)
    smem = pl.BlockSpec(memory_space=pltpu.SMEM)
    hbm = pl.BlockSpec(memory_space=pl.ANY)
    vec, coef, dens = pl.pallas_call(
        functools.partial(kernel, n_sec, n_op),
        out_shape=(
            jax.ShapeDtypeStruct(theta.shape, F32),
            jax.ShapeDtypeStruct((8, 128), F32),
            jax.ShapeDtypeStruct(theta.shape, F32),
        ),
        in_specs=[hbm, hbm, hbm, smem, smem],
        out_specs=(vmem, vmem, vmem),
        scratch_shapes=[
            pltpu.VMEM(theta.shape, F32),
            pltpu.VMEM(left_env.shape, BF16),
            pltpu.VMEM(right_env.shape, BF16),
            pltpu.VMEM((n_sec * sec_dev, width, width), BF16),
            pltpu.VMEM((n_sec * sec_dev, width, width), BF16),
            pltpu.VMEM((STEPS, 3 * sec_dev, width, width), F32),
            pltpu.VMEM((sec_dev, width, width), BF16),
            pltpu.VMEM((n_op, rows, width), BF16),
            pltpu.VMEM((2, n_op, 8, width), F32),
            pltpu.VMEM((2, n_sec, 16, width), F32),
            dma((3, sec_dev)),
            dma((2, n_sec, n_op)),
            dma((n_op,)),
            dma((n_op, n_chip)),
            dma((n_op, n_chip)),
            dma((n_op,)),
            dma((n_op,)),
            dma((n_op,)),
            dma((2, n_op)),
            dma((2, n_op)),
            dma((2, n_sec)),
            dma((2, n_sec)),
        ],
        compiler_params=pltpu.CompilerParams(
            collective_id=0, has_side_effects=True, vmem_limit_bytes=60 * 1024 * 1024
        ),
        cost_estimate=pl.CostEstimate(
            flops=STEPS * 4 * sec_dev * term_dev * width**3,
            bytes_accessed=4 * sec_dev * term_dev * width**2,
            transcendentals=0,
        ),
    )(theta, left_env, right_env, perm, dims)
    return vec, coef[0, :6], dens


def solution(mesh):
    placed = (
        P("sector", None, None),
        P("sector", "op", None, None),
        P("sector", "op", None, None),
        P(),
        P("sector", None),
    )
    return jax.shard_map(
        per_device,
        mesh=mesh,
        in_specs=placed,
        out_specs=(P("sector", None, None), P(), P("sector", None, None)),
        check_vma=False,
    )
```

time: 83.4 us -> 91.8 us (1.10)
  Pallas kernels: 75 us -> 85.1 us
  local copies, waits for them, and re-layouts: 7.47 us -> 5.86 us
    pallas_call x1, Pallas kernels: 75 us -> 85.1 us  [per_device(): pl.pallas_call(functools.partial(kernel, n_sec, n_op), out_shape=(jax.Sha...]
    unnamed x11 -> x3, local copies, waits for them, and re-layouts: 6.96 us -> 4.67 us
where the time goes in v2:
time: 91.8 us; the launch traced here: 91.6 us
  Pallas kernels  85.1 us (93%)
  local copies, waits for them, and re-layouts  5.86 us (6%)
    pallas_call x1, Pallas kernels, per_device(): pl.pallas_call(functools.partial(kernel, n_sec, n_op), out_shape=(jax.Sha...  85.1 us
    unnamed x3, local copies, waits for them, and re-layouts  4.67 us

profile of v2, /device:TPU:0, one launch (start us, length us, event | category | flops | bytes accessed | tf_op | source)
XLA Modules:
  0.0 91.6 jit_solution(9888996192526918696)
XLA Ops:
  0.6 1.3 %copy.8.dims_ref = s32[4,2]{1,0:T(4,128)} copy(s32[4,2]{0,1:T(2,128)} %param.9) | data formatting | bytes 64 | tf_op args[4]
  2.0 85.1 %shard_map.76 = (f32[4,128,128]{2,1,0:T(8,128)}, f32[8,128]{1,0:T(8,128)}, f32[4,128,128]{2,1,0:T(8,128)}) custom-call(f32[4,128,128]{2,1,0:T(8,128)} %theta_hbm.1, bf16[4,16,128,128]{3,2,1,0:T(8,128)(2,1)} %left_hbm.1, bf16[4,16,128,128]{3,2,1,0:T(8,128)(2,1)} %right_hbm.1, s32[32]{0:T(128)} %perm_ref.1, s32[4,2]{1,0:T(4,128)} %copy.8.dims_ref), custom_call_target="tpu_custom_call" | custom-call | flops 1610612736 | bytes 4194304 | tf_op jit(solution)/shard_map/pallas_call | solution.py:310
  87.0 1.2 %slice_bitcast_fusion = f32[6]{0:T(128)} fusion(f32[8,128]{1,0:T(8,128)} %get-tuple-element.7), kind=kLoop, calls=%fused_computation | loop fusion | bytes 48 | tf_op jit(solution)/shard_map/squeeze | solution.py:352
  88.2 1.7 %copy.11 = f32[4,128,128]{2,1,0:T(8,128)} copy(f32[4,128,128]{2,1,0:T(8,128)} %get-tuple-element.12) | data formatting | bytes 524288
  89.9 1.7 %copy.12 = f32[4,128,128]{2,1,0:T(8,128)} copy(f32[4,128,128]{2,1,0:T(8,128)} %get-tuple-element.14) | data formatting | bytes 524288

commit v3 on v2

--- a/solution.py
+++ b/solution.py
@@ -18,7 +18,7 @@
     theta_hbm, left_hbm, right_hbm, perm_ref, dims_ref,
     vec_ref, coef_ref, dens_ref,
     theta_v, left_v, right_v, gath_a, gath_b, basis, pb, rsb, az, ap,
-    env_sem, rsem, zsend, psend, fsend, relay, rs_send, rs_recv,
+    env_sem, rsem, zsend, psend, fsend, zrecv, rs_send, rs_recv,
     az_send, az_recv, ap_send, ap_recv,
 ):
     gath = (gath_a, gath_b)
@@ -31,19 +31,15 @@
     cpb = width // rows
     n_chip = n_sec // 2
     aligned = n_op == sec_dev
-    square = n_chip == 4
+    rounds = ((0, 1), (1, n_op - 1))
 
     s = lax.axis_index("sector")
     z = lax.axis_index("op")
     core = lax.rem(s, 2)
     chip = s // 2
     sib = s + 1 - 2 * core
-    if square:
-        beside = [chip + 1 - 2 * lax.rem(chip, 2), lax.rem(chip + 2, 4), 3 - chip]
-    else:
-        beside = [lax.rem(chip + m, n_chip) for m in range(1, n_chip)]
+    beside = [lax.rem(chip + m, n_chip) for m in range(1, n_chip)]
     peers = [2 * c + core for c in beside]
-    direct = peers[:2] if square else peers
     others = [sib] + [2 * c + 1 - core for c in beside]
     mates = [lax.rem(z + m, n_op) for m in range(1, n_op)]
     plane = [lax.rem(s + m, n_sec) for m in range(1, n_sec)]
@@ -66,15 +62,24 @@
     def block_mask(p, first, n):
         r = lax.broadcasted_iota(jnp.int32, (n, width), 0) + first
         c = lax.broadcasted_iota(jnp.int32, (n, width), 1)
-        return jnp.where((r < dims_ref[p, 0]) & (c < dims_ref[p, 1]), 1.0, 0.0).astype(F32)
+        return jnp.where((r < dims_ref[0, p]) & (c < dims_ref[1, p]), 1.0, 0.0).astype(F32)
 
     def chunk(ref, base, j):
         if cpb == 1:
             return ref.at[base + j]
         return ref.at[base + j // cpb, pl.ds(pl.multiple_of(lax.rem(j, cpb) * rows, rows), rows)]
 
-    def slot(g, owner, j):
-        return chunk(gath[g], owner * sec_dev, j)
+    def slots(g, owner, part):
+        first, n = rounds[part]
+        return gath[g].at[pl.ds(owner * n_op + first, n)]
+
+    def place(block):
+        first = lax.rem(block, sec_dev) * cpb
+        base = lax.div(block, sec_dev) * n_op
+        return [base + lax.rem(first + h - z + n_op, n_op) for h in range(cpb)]
+
+    def load(g, where):
+        return jnp.concatenate([gath[g][w] for w in where], axis=0)
 
     def send(src, dst, ssem, dsem, dev):
         copy = pltpu.make_async_remote_copy(
@@ -96,44 +101,51 @@
     def whole(x):
         return jnp.sum(x, keepdims=True)
 
-    def move(g, j, owner, ssem, dev):
-        return send(slot(g, owner, j), slot(g, owner, j), ssem, rsem.at[g, owner, j], (dev, z))
+    def move(g, owner, part, ssem, dev):
+        ref = slots(g, owner, part)
+        return send(ref, ref, ssem, rsem.at[g, owner, part], (dev, z))
 
     def spread_z(g):
         return [
-            send(slot(g, s, z), slot(g, s, z), zsend.at[i], rsem.at[g, s, z], (s, mate))
-            for i, mate in enumerate(mates)
+            send(
+                gath[g].at[s * n_op], gath[g].at[s * n_op + n_op - i],
+                zsend.at[i - 1], zrecv.at[n_op - i], (s, mate),
+            )
+            for i, mate in enumerate(mates, 1)
         ]
 
-    def spread_plane(g, m, j):
-        return [move(g, j, s, psend.at[m, i], dev) for i, dev in enumerate(direct + [sib])]
-
-    def pass_on(g, m, j):
+    def collect_z(g):
+        for m in range(1, n_op):
+            arrived(gath[g].at[s * n_op + m], zrecv.at[m])
+
+    def spread_plane(g, part):
+        return [move(g, s, part, psend.at[part, i], dev) for i, dev in enumerate(peers + [sib])]
+
+    def pass_on(g, part):
         out = []
         for i, peer in enumerate(peers):
-            arrived(slot(g, peer, j), rsem.at[g, peer, j])
-            if square and i == m % 2:
-                out.append(move(g, j, peer, relay.at[m], peers[1 - i]))
-            out.append(move(g, j, peer, fsend.at[m, i], sib))
+            arrived(slots(g, peer, part), rsem.at[g, peer, part])
+            out.append(move(g, peer, part, fsend.at[part, i], sib))
         return out
 
     def collect(g):
-        for j in [z] + mates:
+        for part in range(2):
             for other in others:
-                arrived(slot(g, other, j), rsem.at[g, other, j])
+                arrived(slots(g, other, part), rsem.at[g, other, part])
 
     own_p = z // cpb
     own_r = pl.multiple_of(lax.rem(z, cpb) * rows, rows)
+    fetch.wait()
     mask = block_mask(own_p, own_r, rows)
-    fetch.wait()
-    for p in range(sec_dev):
-        gath[0][s * sec_dev + p] = (theta_v[p] * block_mask(p, 0, width)).astype(BF16)
+    for m in range(n_op):
+        j = lax.rem(z + m, n_op)
+        p, first = j // cpb, pl.multiple_of(lax.rem(j, cpb) * rows, rows)
+        kept = theta_v[p, pl.ds(first, rows), :] * block_mask(p, first, rows)
+        gath[0][s * n_op + m] = kept.astype(BF16)
 
     pl.semaphore_wait(barrier, n_sec - 1 + n_op - 1)
 
-    sends = []
-    for m, j in enumerate([z] + mates):
-        sends += spread_plane(0, m, j)
+    sends = spread_plane(0, 0) + spread_plane(0, 1)
 
     order = [lax.rem(z + 1 + i, sec_dev) if aligned else i for i in range(sec_dev)]
     wants = []
@@ -150,8 +162,8 @@
 
     src = lax.fori_loop(0, total, look, tuple(jnp.int32(0) for _ in wants))
 
-    for m, j in enumerate([z] + mates):
-        sends += pass_on(0, m, j)
+    src = [place(block) for block in src]
+    sends += pass_on(0, 0) + pass_on(0, 1)
     collect(0)
     for copy in env:
         copy.wait()
@@ -203,7 +215,7 @@
         for i, p in enumerate(order):
             inner = [None] * term_dev
             for c in range(3):
-                x = gath[g][src[3 * i + c]].astype(F32)
+                x = load(g, src[3 * i + c]).astype(F32)
                 if step > 0:
                     x = recur(step, x, 3 * i + c)
                 basis[step, 3 * i + c] = x
@@ -238,17 +250,16 @@
         image = rsb[0].astype(F32)
         for j in range(1, n_op):
             image = image + rsb[j].astype(F32)
-        slot(nxt, s, z)[...] = (image * mask).astype(BF16)
+        gath[nxt][s * n_op] = (image * mask).astype(BF16)
         sends = spread_z(nxt)
         last = step == STEPS - 1
         if not last:
-            sends += spread_plane(nxt, 0, z)
+            sends += spread_plane(nxt, 0)
         small += share_plane(use, jnp.concatenate([add_op(use), rr], axis=0))
         if not last:
-            for m, j in enumerate(mates):
-                arrived(slot(nxt, s, j), rsem.at[nxt, s, j])
-                sends += spread_plane(nxt, m + 1, j)
-            sends += pass_on(nxt, 0, z)
+            collect_z(nxt)
+            sends += spread_plane(nxt, 1)
+            sends += pass_on(nxt, 0)
         a_sum, n_sum = add_plane(use)
         norm = jnp.sqrt(n_sum / count + 1e-06)
         inv = 1.0 / norm
@@ -260,19 +271,17 @@
         last_inv = inv
         alphas.append(alpha)
         if not last:
-            for m, j in enumerate(mates):
-                sends += pass_on(nxt, m + 1, j)
+            sends += pass_on(nxt, 1)
         for copy in rs + small:
             copy.wait_send()
         if not last:
             collect(nxt)
 
     g, use = STEPS % 2, STEPS % 2
-    for mate in mates:
-        arrived(slot(g, s, mate), rsem.at[g, s, mate])
+    collect_z(g)
     rr = jnp.zeros((8, width), F32)
     for i, p in enumerate(order):
-        u = recur(STEPS, gath[g][s * sec_dev + p].astype(F32), 3 * i + own_c)
+        u = recur(STEPS, load(g, place(s * sec_dev + p)).astype(F32), 3 * i + own_c)
         theta_v[p] = u
         pb[p] = u.astype(BF16)
     for p in range(sec_dev):
@@ -306,7 +315,7 @@
     dma = pltpu.SemaphoreType.DMA
     vmem = pl.BlockSpec(memory_space=pltpu.VMEM)
     smem = pl.BlockSpec(memory_space=pltpu.SMEM)
-    hbm = pl.BlockSpec(memory_space=pl.ANY)
+    hbm = pl.BlockSpec(memory_space=pltpu.HBM)
     vec, coef, dens = pl.pallas_call(
         functools.partial(kernel, n_sec, n_op),
         out_shape=(
@@ -320,18 +329,18 @@
             pltpu.VMEM(theta.shape, F32),
             pltpu.VMEM(left_env.shape, BF16),
             pltpu.VMEM(right_env.shape, BF16),
-            pltpu.VMEM((n_sec * sec_dev, width, width), BF16),
-            pltpu.VMEM((n_sec * sec_dev, width, width), BF16),
+            pltpu.VMEM((n_sec * n_op, rows, width), BF16),
+            pltpu.VMEM((n_sec * n_op, rows, width), BF16),
             pltpu.VMEM((STEPS, 3 * sec_dev, width, width), F32),
             pltpu.VMEM((sec_dev, width, width), BF16),
             pltpu.VMEM((n_op, rows, width), BF16),
             pltpu.VMEM((2, n_op, 8, width), F32),
             pltpu.VMEM((2, n_sec, 16, width), F32),
             dma((3, sec_dev)),
-            dma((2, n_sec, n_op)),
+            dma((2, n_sec, 2)),
             dma((n_op,)),
-            dma((n_op, n_chip)),
-            dma((n_op, n_chip)),
+            dma((2, n_chip)),
+            dma((2, n_chip)),
             dma((n_op,)),
             dma((n_op,)),
             dma((n_op,)),
@@ -341,14 +350,14 @@
             dma((2, n_sec)),
         ],
         compiler_params=pltpu.CompilerParams(
-            collective_id=0, has_side_effects=True, vmem_limit_bytes=60 * 1024 * 1024
+            collective_id=0, has_side_effects=True, vmem_limit_bytes=53 * 1024 * 1024
         ),
         cost_estimate=pl.CostEstimate(
             flops=STEPS * 4 * sec_dev * term_dev * width**3,
             bytes_accessed=4 * sec_dev * term_dev * width**2,
             transcendentals=0,
         ),
-    )(theta, left_env, right_env, perm, dims)
+    )(theta, left_env, right_env, perm, dims.T)
     return vec, coef[0, :6], dens
 
 

time: 91.8 us -> 69.8 us (0.76)
  Pallas kernels: 85.1 us -> 64.8 us
  local copies, waits for them, and re-layouts: 5.86 us -> 4.19 us
    pallas_call x1, Pallas kernels: 85.1 us -> 64.8 us  [per_device(): pl.pallas_call(functools.partial(kernel, n_sec, n_op), out_shape=(jax.Sha...]
    unnamed x3 -> x8, local copies, waits for them, and re-layouts: 4.67 us -> 3.68 us
where the time goes in v3:
time: 69.8 us; the launch traced here: 69.6 us
  Pallas kernels  64.8 us (93%)
  local copies, waits for them, and re-layouts  4.19 us (6%)
    pallas_call x1, Pallas kernels, per_device(): pl.pallas_call(functools.partial(kernel, n_sec, n_op), out_shape=(jax.Sha...  64.8 us
    unnamed x8, local copies, waits for them, and re-layouts  3.68 us

profile of v3, /device:TPU:0, one launch (start us, length us, event | category | flops | bytes accessed | tf_op | source)
XLA Modules:
  0.0 69.6 jit_solution(7291813325907602531)
XLA Ops:
  0.6 0.0 copy-start
  0.6 0.9 %copy-done = f32[4,128,128]{2,1,0:T(8,128)S(1)} copy-done((f32[4,128,128]{2,1,0:T(8,128)S(1)}, f32[4,128,128]{2,1,0:T(8,128)}, u32[]{:S(2)}) %copy-start) | copy-done | bytes 262168
  1.6 0.0 copy-start.1
  1.6 0.7 copy-done.1
  2.3 0.0 copy-start.2
  2.3 0.7 copy-done.2
  2.9 64.8 %shard_map.76 = (f32[4,128,128]{2,1,0:T(8,128)S(1)}, f32[8,128]{1,0:T(8,128)S(1)}, f32[4,128,128]{2,1,0:T(8,128)S(1)}) custom-call(f32[4,128,128]{2,1,0:T(8,128)S(1)} %copy-done, bf16[4,16,128,128]{3,2,1,0:T(8,128)(2,1)} %left_hbm.1, bf16[4,16,128,128]{3,2,1,0:T(8,128)(2,1)} %right_hbm.1, s32[32]{0:T(128)S(1)} %copy-done.2, s32[2,4]{1,0:T(2,128)S(1)} %bitcast.3), custom_call_target="tpu_custom_call" | custom-call | flops 1610612736 | bytes 4194304 | tf_op jit(solution)/shard_map/pallas_call | solution.py:319
  67.7 0.5 slice_bitcast_fusion
  68.2 0.7 %copy.10 = f32[4,128,128]{2,1,0:T(8,128)} copy(f32[4,128,128]{2,1,0:T(8,128)S(1)} %get-tuple-element.12) | data formatting | bytes 524288
  68.9 0.7 %copy.11 = f32[4,128,128]{2,1,0:T(8,128)} copy(f32[4,128,128]{2,1,0:T(8,128)S(1)} %get-tuple-element.14) | data formatting | bytes 524288
Async XLA Ops:
  0.6 1.0 %copy-start = (f32[4,128,128]{2,1,0:T(8,128)S(1)}, f32[4,128,128]{2,1,0:T(8,128)}, u32[]{:S(2)}) copy-start(f32[4,128,128]{2,1,0:T(8,128)} %theta_hbm.1) | copy-start | bytes 786436
  1.6 0.7 copy-start.1
  2.3 0.7 copy-start.2

commit v4 on v3

--- a/solution.py
+++ b/solution.py
@@ -17,7 +17,7 @@
     n_sec, n_op,
     theta_hbm, left_hbm, right_hbm, perm_ref, dims_ref,
     vec_ref, coef_ref, dens_ref,
-    theta_v, left_v, right_v, gath_a, gath_b, basis, pb, rsb, az, ap,
+    theta_v, left_v, right_v, gath_a, gath_b, basis, mid, pb, rsb, az, ap,
     env_sem, rsem, zsend, psend, fsend, zrecv, rs_send, rs_recv,
     az_send, az_recv, ap_send, ap_recv,
 ):
@@ -133,6 +133,43 @@
             for other in others:
                 arrived(slots(g, other, part), rsem.at[g, other, part])
 
+    weights = []
+    def recur(k, block, where):
+        value = block * weights[-1][0] + basis[k - 1, where] * weights[-1][1]
+        if k > 1:
+            value = value + basis[k - 2, where] * weights[-1][2]
+        return value
+
+    per_class = term_dev // 3
+
+    def own_place(p):
+        return [s * n_op + lax.rem(p * cpb + h - z + n_op, n_op) for h in range(cpb)]
+
+    def class_terms(q):
+        first = lax.rem(3 * term_dev * n_op + q - z * term_dev, 3)
+        return [first + 3 * n for n in range(per_class)]
+
+    def left_products(p, terms, x):
+        lhs = jnp.concatenate([left_v[p, t] for t in terms], axis=0)
+        got = jnp.dot(lhs, x, preferred_element_type=F32).astype(BF16)
+        return [got[n * width:(n + 1) * width] for n in range(len(terms))]
+
+    def right_products(p, terms, inner):
+        return jnp.dot(
+            jnp.concatenate(inner, axis=1),
+            jnp.concatenate([right_v[p, t] for t in terms], axis=0),
+            preferred_element_type=F32,
+        )
+
+    def own_products(step, g):
+        for i, p in enumerate(order):
+            x = load(g, own_place(p)).astype(F32)
+            if step > 0:
+                x = recur(step, x, 3 * i + 1)
+            basis[step, 3 * i + 1] = x
+            terms = class_terms(1)
+            mid[i] = right_products(p, terms, left_products(p, terms, x.astype(BF16)))
+
     own_p = z // cpb
     own_r = pl.multiple_of(lax.rem(z, cpb) * rows, rows)
     fetch.wait()
@@ -151,10 +188,7 @@
     wants = []
     for p in order:
         mine = perm_ref[s * sec_dev + p]
-        for c in range(3):
-            q = lax.rem(z * term_dev + c, 3)
-            wants.append(lax.rem(mine + q - 1 + total, total))
-    own_c = lax.rem(3 * term_dev * n_op + 1 - z * term_dev, 3)
+        wants += [lax.rem(mine + total - 1, total), lax.rem(mine + 1, total)]
 
     def look(i, found):
         here = perm_ref[i]
@@ -163,10 +197,12 @@
     src = lax.fori_loop(0, total, look, tuple(jnp.int32(0) for _ in wants))
 
     src = [place(block) for block in src]
-    sends += pass_on(0, 0) + pass_on(0, 1)
-    collect(0)
+    sends += pass_on(0, 0)
     for copy in env:
         copy.wait()
+    own_products(0, 0)
+    sends += pass_on(0, 1)
+    collect(0)
 
     def share(use):
         return [
@@ -197,13 +233,6 @@
             acc = acc + ap[use, j]
         return whole(acc[0:8]), whole(acc[8:16])
 
-    def recur(k, block, where):
-        value = block * weights[0] + basis[k - 1, where] * weights[1]
-        if k > 1:
-            value = value + basis[k - 2, where] * weights[2]
-        return value
-
-    weights = None
     last_inv = None
     alphas, betas = [], []
     for step in range(STEPS):
@@ -213,24 +242,21 @@
         rr = jnp.zeros((8, width), F32)
         rs = []
         for i, p in enumerate(order):
-            inner = [None] * term_dev
-            for c in range(3):
-                x = load(g, src[3 * i + c]).astype(F32)
+            inner, terms = [], []
+            for q in (0, 2):
+                x = load(g, src[2 * i + q // 2]).astype(F32)
                 if step > 0:
-                    x = recur(step, x, 3 * i + c)
-                basis[step, 3 * i + c] = x
-                terms = list(range(c, term_dev, 3))
-                lhs = jnp.concatenate([left_v[p, t] for t in terms], axis=0)
-                got = jnp.dot(lhs, x.astype(BF16), preferred_element_type=F32).astype(BF16)
-                for n, t in enumerate(terms):
-                    inner[t] = got[n * width:(n + 1) * width]
-            part = jnp.dot(
-                jnp.concatenate(inner, axis=1),
-                right_v[p].reshape(term_dev * width, width),
-                preferred_element_type=F32,
-            )
+                    x = recur(step, x, 3 * i + q)
+                basis[step, 3 * i + q] = x
+                terms += class_terms(q)
+                inner += left_products(p, class_terms(q), x.astype(BF16))
+            for t in range(3 * per_class, term_dev):
+                x = basis[step, 3 * i + lax.rem(z * term_dev + t, 3)]
+                terms.append(t)
+                inner += left_products(p, [t], x.astype(BF16))
+            part = mid[i] + right_products(p, terms, inner)
             pb[p] = part.astype(BF16)
-            dot_acc = dot_acc + fold(part * basis[step, 3 * i + own_c])
+            dot_acc = dot_acc + fold(part * basis[step, 3 * i + 1])
             if aligned and i < sec_dev - 1:
                 rs.append(send(pb.at[p], rsb.at[z], rs_send.at[i], rs_recv.at[z], (s, p)))
         if not aligned:
@@ -238,7 +264,7 @@
                 rs.append(send(chunk(pb, 0, mate), rsb.at[z], rs_send.at[i], rs_recv.at[z], (s, mate)))
         for p in range(sec_dev):
             i = lax.rem(p + 2 * sec_dev - 1 - z, sec_dev) if aligned else p
-            own = basis[step, 3 * i + own_c]
+            own = basis[step, 3 * i + 1]
             rr = rr + fold(own * own)
         az[use, z] = dot_acc
         small = share(use)
@@ -264,13 +290,14 @@
         norm = jnp.sqrt(n_sum / count + 1e-06)
         inv = 1.0 / norm
         alpha = a_sum * (scale / count) * inv * inv
-        weights = [inv * scale, -alpha * inv]
+        weights.append([inv * scale, -alpha * inv])
         if step > 0:
-            weights.append(-norm * last_inv)
+            weights[-1].append(-norm * last_inv)
             betas.append(norm)
         last_inv = inv
         alphas.append(alpha)
         if not last:
+            own_products(step + 1, nxt)
             sends += pass_on(nxt, 1)
         for copy in rs + small:
             copy.wait_send()
@@ -281,7 +308,7 @@
     collect_z(g)
     rr = jnp.zeros((8, width), F32)
     for i, p in enumerate(order):
-        u = recur(STEPS, load(g, place(s * sec_dev + p)).astype(F32), 3 * i + own_c)
+        u = recur(STEPS, load(g, own_place(p)).astype(F32), 3 * i + 1)
         theta_v[p] = u
         pb[p] = u.astype(BF16)
     for p in range(sec_dev):
@@ -332,6 +359,7 @@
             pltpu.VMEM((n_sec * n_op, rows, width), BF16),
             pltpu.VMEM((n_sec * n_op, rows, width), BF16),
             pltpu.VMEM((STEPS, 3 * sec_dev, width, width), F32),
+            pltpu.VMEM((sec_dev, width, width), F32),
             pltpu.VMEM((sec_dev, width, width), BF16),
             pltpu.VMEM((n_op, rows, width), BF16),
             pltpu.VMEM((2, n_op, 8, width), F32),

time: 69.8 us -> 69 us (0.989)
  Pallas kernels: 64.8 us -> 64 us
    pallas_call x1, Pallas kernels: 64.8 us -> 64 us  [per_device(): pl.pallas_call(functools.partial(kernel, n_sec, n_op), out_shape=(jax.Sha...]
where the time goes in v4:
time: 69 us; the launch traced here: 68.8 us
  Pallas kernels  64 us (93%)
  local copies, waits for them, and re-layouts  4.19 us (6%)
    pallas_call x1, Pallas kernels, per_device(): pl.pallas_call(functools.partial(kernel, n_sec, n_op), out_shape=(jax.Sha...  64 us
    unnamed x8, local copies, waits for them, and re-layouts  3.68 us

profile of v4, /device:TPU:0, one launch (start us, length us, event | category | flops | bytes accessed | tf_op | source)
XLA Modules:
  0.0 68.8 jit_solution(1566229867033043926)
XLA Ops:
  0.6 0.0 copy-start
  0.6 0.9 %copy-done = f32[4,128,128]{2,1,0:T(8,128)S(1)} copy-done((f32[4,128,128]{2,1,0:T(8,128)S(1)}, f32[4,128,128]{2,1,0:T(8,128)}, u32[]{:S(2)}) %copy-start) | copy-done | bytes 262168
  1.6 0.0 copy-start.1
  1.6 0.7 copy-done.1
  2.3 0.0 copy-start.2
  2.3 0.7 copy-done.2
  2.9 64.0 %shard_map.76 = (f32[4,128,128]{2,1,0:T(8,128)S(1)}, f32[8,128]{1,0:T(8,128)S(1)}, f32[4,128,128]{2,1,0:T(8,128)S(1)}) custom-call(f32[4,128,128]{2,1,0:T(8,128)S(1)} %copy-done, bf16[4,16,128,128]{3,2,1,0:T(8,128)(2,1)} %left_hbm.1, bf16[4,16,128,128]{3,2,1,0:T(8,128)(2,1)} %right_hbm.1, s32[32]{0:T(128)S(1)} %copy-done.2, s32[2,4]{1,0:T(2,128)S(1)} %bitcast.3), custom_call_target="tpu_custom_call" | custom-call | flops 1610612736 | bytes 4194304 | tf_op jit(solution)/shard_map/pallas_call | solution.py:346
  66.9 0.5 slice_bitcast_fusion
  67.4 0.7 %copy.10 = f32[4,128,128]{2,1,0:T(8,128)} copy(f32[4,128,128]{2,1,0:T(8,128)S(1)} %get-tuple-element.12) | data formatting | bytes 524288
  68.1 0.7 %copy.11 = f32[4,128,128]{2,1,0:T(8,128)} copy(f32[4,128,128]{2,1,0:T(8,128)S(1)} %get-tuple-element.14) | data formatting | bytes 524288
Async XLA Ops:
  0.6 1.0 %copy-start = (f32[4,128,128]{2,1,0:T(8,128)S(1)}, f32[4,128,128]{2,1,0:T(8,128)}, u32[]{:S(2)}) copy-start(f32[4,128,128]{2,1,0:T(8,128)} %theta_hbm.1) | copy-start | bytes 786436
  1.6 0.7 copy-start.1
  2.3 0.7 copy-start.2

commit v5 on v4

--- a/solution.py
+++ b/solution.py
@@ -31,7 +31,14 @@
     cpb = width // rows
     n_chip = n_sec // 2
     aligned = n_op == sec_dev
-    rounds = ((0, 1), (1, n_op - 1))
+    groups = ((0, n_op - 1), (n_op - 1, 1))
+
+    def xor(a, b):
+        out = 0
+        for k in range(n_op.bit_length() - 1):
+            bit = 1 << k
+            out = out + bit * lax.rem(lax.div(a, bit) + (b // bit if isinstance(b, int) else lax.div(b, bit)), 2)
+        return out
 
     s = lax.axis_index("sector")
     z = lax.axis_index("op")
@@ -41,7 +48,7 @@
     beside = [lax.rem(chip + m, n_chip) for m in range(1, n_chip)]
     peers = [2 * c + core for c in beside]
     others = [sib] + [2 * c + 1 - core for c in beside]
-    mates = [lax.rem(z + m, n_op) for m in range(1, n_op)]
+    mates = [xor(z, m) for m in range(1, n_op)]
     plane = [lax.rem(s + m, n_sec) for m in range(1, n_sec)]
 
     fetch = pltpu.make_async_copy(theta_hbm, theta_v, env_sem.at[2, 0])
@@ -69,14 +76,13 @@
             return ref.at[base + j]
         return ref.at[base + j // cpb, pl.ds(pl.multiple_of(lax.rem(j, cpb) * rows, rows), rows)]
 
-    def slots(g, owner, part):
-        first, n = rounds[part]
+    def slots(g, owner, first, n):
         return gath[g].at[pl.ds(owner * n_op + first, n)]
 
     def place(block):
         first = lax.rem(block, sec_dev) * cpb
         base = lax.div(block, sec_dev) * n_op
-        return [base + lax.rem(first + h - z + n_op, n_op) for h in range(cpb)]
+        return [base + xor(z, first + h) for h in range(cpb)]
 
     def load(g, where):
         return jnp.concatenate([gath[g][w] for w in where], axis=0)
@@ -101,37 +107,37 @@
     def whole(x):
         return jnp.sum(x, keepdims=True)
 
-    def move(g, owner, part, ssem, dev):
-        ref = slots(g, owner, part)
-        return send(ref, ref, ssem, rsem.at[g, owner, part], (dev, z))
+    def move(g, owner, span, ssem, k, dev):
+        ref = slots(g, owner, *span)
+        return send(ref, ref, ssem, rsem.at[g, owner, k], (dev, z))
 
     def spread_z(g):
         return [
-            send(
-                gath[g].at[s * n_op], gath[g].at[s * n_op + n_op - i],
-                zsend.at[i - 1], zrecv.at[n_op - i], (s, mate),
-            )
-            for i, mate in enumerate(mates, 1)
+            send(gath[g].at[s * n_op], gath[g].at[s * n_op + m], zsend.at[m], zrecv.at[m], (s, mate))
+            for m, mate in enumerate(mates, 1)
         ]
 
-    def collect_z(g):
-        for m in range(1, n_op):
-            arrived(gath[g].at[s * n_op + m], zrecv.at[m])
-
-    def spread_plane(g, part):
-        return [move(g, s, part, psend.at[part, i], dev) for i, dev in enumerate(peers + [sib])]
-
-    def pass_on(g, part):
+    def collect_z(g, m):
+        arrived(gath[g].at[s * n_op + m], zrecv.at[m])
+
+    def spread_plane(g, span, k):
+        return [move(g, s, span, psend.at[k, i], k, peer) for i, peer in enumerate(peers)]
+
+    def spread_chip(g, k):
+        return [move(g, s, groups[k], psend.at[k, n_chip - 1], k, sib)]
+
+    def pass_on(g, k, spans):
         out = []
         for i, peer in enumerate(peers):
-            arrived(slots(g, peer, part), rsem.at[g, peer, part])
-            out.append(move(g, peer, part, fsend.at[part, i], sib))
+            for j, span in spans:
+                arrived(slots(g, peer, *span), rsem.at[g, peer, j])
+            out.append(move(g, peer, groups[k], fsend.at[k, i], k, sib))
         return out
 
     def collect(g):
-        for part in range(2):
+        for k in range(2):
             for other in others:
-                arrived(slots(g, other, part), rsem.at[g, other, part])
+                arrived(slots(g, other, *groups[k]), rsem.at[g, other, k])
 
     weights = []
     def recur(k, block, where):
@@ -143,7 +149,7 @@
     per_class = term_dev // 3
 
     def own_place(p):
-        return [s * n_op + lax.rem(p * cpb + h - z + n_op, n_op) for h in range(cpb)]
+        return [s * n_op + xor(z, p * cpb + h) for h in range(cpb)]
 
     def class_terms(q):
         first = lax.rem(3 * term_dev * n_op + q - z * term_dev, 3)
@@ -175,16 +181,18 @@
     fetch.wait()
     mask = block_mask(own_p, own_r, rows)
     for m in range(n_op):
-        j = lax.rem(z + m, n_op)
-        p, first = j // cpb, pl.multiple_of(lax.rem(j, cpb) * rows, rows)
+        j = xor(z, m)
+        p, first = lax.div(j, cpb), pl.multiple_of(lax.rem(j, cpb) * rows, rows)
         kept = theta_v[p, pl.ds(first, rows), :] * block_mask(p, first, rows)
         gath[0][s * n_op + m] = kept.astype(BF16)
 
     pl.semaphore_wait(barrier, n_sec - 1 + n_op - 1)
 
-    sends = spread_plane(0, 0) + spread_plane(0, 1)
-
-    order = [lax.rem(z + 1 + i, sec_dev) if aligned else i for i in range(sec_dev)]
+    sends = []
+    for k in range(2):
+        sends += spread_plane(0, groups[k], k) + spread_chip(0, k)
+
+    order = [xor(z, sec_dev - 1 - i) if aligned else i for i in range(sec_dev)]
     wants = []
     for p in order:
         mine = perm_ref[s * sec_dev + p]
@@ -197,11 +205,11 @@
     src = lax.fori_loop(0, total, look, tuple(jnp.int32(0) for _ in wants))
 
     src = [place(block) for block in src]
-    sends += pass_on(0, 0)
+    for k in range(2):
+        sends += pass_on(0, k, [(k, groups[k])])
     for copy in env:
         copy.wait()
     own_products(0, 0)
-    sends += pass_on(0, 1)
     collect(0)
 
     def share(use):
@@ -263,7 +271,7 @@
             for i, mate in enumerate(mates):
                 rs.append(send(chunk(pb, 0, mate), rsb.at[z], rs_send.at[i], rs_recv.at[z], (s, mate)))
         for p in range(sec_dev):
-            i = lax.rem(p + 2 * sec_dev - 1 - z, sec_dev) if aligned else p
+            i = sec_dev - 1 - xor(z, p) if aligned else p
             own = basis[step, 3 * i + 1]
             rr = rr + fold(own * own)
         az[use, z] = dot_acc
@@ -280,12 +288,15 @@
         sends = spread_z(nxt)
         last = step == STEPS - 1
         if not last:
-            sends += spread_plane(nxt, 0)
+            sends += spread_plane(nxt, (0, 1), 0)
         small += share_plane(use, jnp.concatenate([add_op(use), rr], axis=0))
         if not last:
-            collect_z(nxt)
-            sends += spread_plane(nxt, 1)
-            sends += pass_on(nxt, 0)
+            for m in range(1, n_op):
+                collect_z(nxt, m)
+                sends += spread_plane(nxt, (m, 1), m)
+                if m >= n_op - 2:
+                    sends += spread_chip(nxt, m - n_op + 2)
+            sends += pass_on(nxt, 0, [(m, (m, 1)) for m in range(n_op - 1)])
         a_sum, n_sum = add_plane(use)
         norm = jnp.sqrt(n_sum / count + 1e-06)
         inv = 1.0 / norm
@@ -297,15 +308,16 @@
         last_inv = inv
         alphas.append(alpha)
         if not last:
+            sends += pass_on(nxt, 1, [(n_op - 1, (n_op - 1, 1))])
             own_products(step + 1, nxt)
-            sends += pass_on(nxt, 1)
         for copy in rs + small:
             copy.wait_send()
         if not last:
             collect(nxt)
 
     g, use = STEPS % 2, STEPS % 2
-    collect_z(g)
+    for m in range(1, n_op):
+        collect_z(g, m)
     rr = jnp.zeros((8, width), F32)
     for i, p in enumerate(order):
         u = recur(STEPS, load(g, own_place(p)).astype(F32), 3 * i + 1)
@@ -365,9 +377,9 @@
             pltpu.VMEM((2, n_op, 8, width), F32),
             pltpu.VMEM((2, n_sec, 16, width), F32),
             dma((3, sec_dev)),
-            dma((2, n_sec, 2)),
+            dma((2, n_sec, n_op)),
             dma((n_op,)),
-            dma((2, n_chip)),
+            dma((n_op, n_chip)),
             dma((2, n_chip)),
             dma((n_op,)),
             dma((n_op,)),
@@ -378,7 +390,7 @@
             dma((2, n_sec)),
         ],
         compiler_params=pltpu.CompilerParams(
-            collective_id=0, has_side_effects=True, vmem_limit_bytes=53 * 1024 * 1024
+            collective_id=0, has_side_effects=True, vmem_limit_bytes=54580 * 1024
         ),
         cost_estimate=pl.CostEstimate(
             flops=STEPS * 4 * sec_dev * term_dev * width**3,

time: 69 us -> 65.9 us (0.955)
  Pallas kernels: 64 us -> 61.8 us
  local copies, waits for them, and re-layouts: 4.19 us -> 3.24 us
    pallas_call x1, Pallas kernels: 64 us -> 61.8 us  [per_device(): pl.pallas_call(functools.partial(kernel, n_sec, n_op), out_shape=(jax.Sha...]
    unnamed x8 -> x6, local copies, waits for them, and re-layouts: 3.68 us -> 2.73 us
where the time goes in v5:
time: 65.9 us; the launch traced here: 65.7 us
  Pallas kernels  61.8 us (94%)
  local copies, waits for them, and re-layouts  3.24 us (5%)
    pallas_call x1, Pallas kernels, per_device(): pl.pallas_call(functools.partial(kernel, n_sec, n_op), out_shape=(jax.Sha...  61.8 us
    unnamed x6, local copies, waits for them, and re-layouts  2.73 us

profile of v5, /device:TPU:0, one launch (start us, length us, event | category | flops | bytes accessed | tf_op | source)
XLA Modules:
  0.0 65.7 jit_solution(13648817204257292639)
XLA Ops:
  0.6 0.0 copy-start
  0.6 0.7 %copy-done = s32[4,2]{0,1:T(2,128)S(1)} copy-done((s32[4,2]{0,1:T(2,128)S(1)}, s32[4,2]{0,1:T(2,128)}, u32[]{:S(2)}) %copy-start) | copy-done | bytes 56
  1.3 0.0 copy-start.1
  1.3 0.7 copy-done.1
  2.0 61.8 %shard_map.76 = (f32[4,128,128]{2,1,0:T(8,128)S(1)}, f32[8,128]{1,0:T(8,128)S(1)}, f32[4,128,128]{2,1,0:T(8,128)S(1)}) custom-call(f32[4,128,128]{2,1,0:T(8,128)} %theta_hbm.1, bf16[4,16,128,128]{3,2,1,0:T(8,128)(2,1)} %left_hbm.1, bf16[4,16,128,128]{3,2,1,0:T(8,128)(2,1)} %right_hbm.1, s32[32]{0:T(128)S(1)} %copy-done.1, s32[2,4]{1,0:T(2,128)S(1)} %bitcast.3), custom_call_target="tpu_custom_call" | custom-call | flops 1610612736 | bytes 4194304 | tf_op jit(solution)/shard_map/pallas_call | solution.py:358
  63.8 0.5 slice_bitcast_fusion
  64.3 0.7 %copy.10 = f32[4,128,128]{2,1,0:T(8,128)} copy(f32[4,128,128]{2,1,0:T(8,128)S(1)} %get-tuple-element.12) | data formatting | bytes 524288
  65.0 0.7 %copy.11 = f32[4,128,128]{2,1,0:T(8,128)} copy(f32[4,128,128]{2,1,0:T(8,128)S(1)} %get-tuple-element.14) | data formatting | bytes 524288
Async XLA Ops:
  0.6 0.7 %copy-start = (s32[4,2]{0,1:T(2,128)S(1)}, s32[4,2]{0,1:T(2,128)}, u32[]{:S(2)}) copy-start(s32[4,2]{0,1:T(2,128)} %param.9) | copy-start | bytes 100
  1.3 0.7 copy-start.1

commit v6 on v5

--- a/solution.py
+++ b/solution.py
@@ -18,7 +18,7 @@
     theta_hbm, left_hbm, right_hbm, perm_ref, dims_ref,
     vec_ref, coef_ref, dens_ref,
     theta_v, left_v, right_v, gath_a, gath_b, basis, mid, pb, rsb, az, ap,
-    env_sem, rsem, zsend, psend, fsend, zrecv, rs_send, rs_recv,
+    env_sem, rsem, zsend, psend, fsend, zrecv, pass_sem, rs_send, rs_recv,
     az_send, az_recv, ap_send, ap_recv,
 ):
     gath = (gath_a, gath_b)
@@ -31,7 +31,9 @@
     cpb = width // rows
     n_chip = n_sec // 2
     aligned = n_op == sec_dev
-    groups = ((0, n_op - 1), (n_op - 1, 1))
+    half = n_op // 2
+    groups = ((0, half), (half, n_op - half))
+    square = n_chip == 4
 
     def xor(a, b):
         out = 0
@@ -45,8 +47,13 @@
     core = lax.rem(s, 2)
     chip = s // 2
     sib = s + 1 - 2 * core
-    beside = [lax.rem(chip + m, n_chip) for m in range(1, n_chip)]
+    if square:
+        beside = [chip + 1 - 2 * lax.rem(chip, 2), lax.rem(chip + 2, 4), 3 - chip]
+    else:
+        beside = [lax.rem(chip + m, n_chip) for m in range(1, n_chip)]
     peers = [2 * c + core for c in beside]
+    near = [0, 1] if square else list(range(n_chip - 1))
+    far = [2] if square else []
     others = [sib] + [2 * c + 1 - core for c in beside]
     mates = [xor(z, m) for m in range(1, n_op)]
     plane = [lax.rem(s + m, n_sec) for m in range(1, n_sec)]
@@ -121,17 +128,29 @@
         arrived(gath[g].at[s * n_op + m], zrecv.at[m])
 
     def spread_plane(g, span, k):
-        return [move(g, s, span, psend.at[k, i], k, peer) for i, peer in enumerate(peers)]
+        return [move(g, s, span, psend.at[k, i], k, peers[i]) for i in near]
 
     def spread_chip(g, k):
         return [move(g, s, groups[k], psend.at[k, n_chip - 1], k, sib)]
 
-    def pass_on(g, k, spans):
+    def take(g, i, j, span, done):
+        if (i, j) not in done:
+            done.add((i, j))
+            arrived(slots(g, peers[i], *span), rsem.at[g, peers[i], j])
+
+    def relay(g, j, first, span, done):
+        if not square:
+            return []
+        i = 0 if first else 1
+        take(g, i, j, span, done)
+        return [move(g, peers[i], span, pass_sem.at[j], j, peers[1 - i])]
+
+    def pass_on(g, k, who, spans, done):
         out = []
-        for i, peer in enumerate(peers):
+        for i in who:
             for j, span in spans:
-                arrived(slots(g, peer, *span), rsem.at[g, peer, j])
-            out.append(move(g, peer, groups[k], fsend.at[k, i], k, sib))
+                take(g, i, j, span, done)
+            out.append(move(g, peers[i], groups[k], fsend.at[k, i], k, sib))
         return out
 
     def collect(g):
@@ -205,8 +224,12 @@
     src = lax.fori_loop(0, total, look, tuple(jnp.int32(0) for _ in wants))
 
     src = [place(block) for block in src]
+    done = set()
     for k in range(2):
-        sends += pass_on(0, k, [(k, groups[k])])
+        sends += relay(0, k, k == 0, groups[k], done)
+    for who in (near, far):
+        for k in range(2):
+            sends += pass_on(0, k, who, [(k, groups[k])], done)
     for copy in env:
         copy.wait()
     own_products(0, 0)
@@ -291,12 +314,19 @@
             sends += spread_plane(nxt, (0, 1), 0)
         small += share_plane(use, jnp.concatenate([add_op(use), rr], axis=0))
         if not last:
+            done = set()
+            spans = [[(m, (m, 1)) for m in range(a, a + n)] for a, n in groups]
             for m in range(1, n_op):
                 collect_z(nxt, m)
                 sends += spread_plane(nxt, (m, 1), m)
-                if m >= n_op - 2:
-                    sends += spread_chip(nxt, m - n_op + 2)
-            sends += pass_on(nxt, 0, [(m, (m, 1)) for m in range(n_op - 1)])
+                if m == half - 1 or m == n_op - 1:
+                    sends += spread_chip(nxt, m // half)
+                if m >= 2:
+                    sends += relay(nxt, m - 2, m - 2 < half, (m - 2, 1), done)
+            for m in range(n_op - 2, n_op):
+                sends += relay(nxt, m, m < half, (m, 1), done)
+            for k in range(2):
+                sends += pass_on(nxt, k, near, spans[k], done)
         a_sum, n_sum = add_plane(use)
         norm = jnp.sqrt(n_sum / count + 1e-06)
         inv = 1.0 / norm
@@ -308,7 +338,8 @@
         last_inv = inv
         alphas.append(alpha)
         if not last:
-            sends += pass_on(nxt, 1, [(n_op - 1, (n_op - 1, 1))])
+            for k in range(2):
+                sends += pass_on(nxt, k, far, spans[k], done)
             own_products(step + 1, nxt)
         for copy in rs + small:
             copy.wait_send()
@@ -384,6 +415,7 @@
             dma((n_op,)),
             dma((n_op,)),
             dma((n_op,)),
+            dma((n_op,)),
             dma((2, n_op)),
             dma((2, n_op)),
             dma((2, n_sec)),

time: 65.9 us -> 69.6 us (1.056)
  Pallas kernels: 61.8 us -> 65.6 us
    pallas_call x1, Pallas kernels: 61.8 us -> 65.6 us  [per_device(): pl.pallas_call(functools.partial(kernel, n_sec, n_op), out_shape=(jax.Sha...]
where the time goes in v6:
time: 69.6 us; the launch traced here: 69.5 us
  Pallas kernels  65.6 us (94%)
  local copies, waits for them, and re-layouts  3.24 us (5%)
    pallas_call x1, Pallas kernels, per_device(): pl.pallas_call(functools.partial(kernel, n_sec, n_op), out_shape=(jax.Sha...  65.6 us
    unnamed x6, local copies, waits for them, and re-layouts  2.73 us

profile of v6, /device:TPU:0, one launch (start us, length us, event | category | flops | bytes accessed | tf_op | source)
XLA Modules:
  0.0 69.5 jit_solution(3578767475367223560)
XLA Ops:
  0.6 0.0 copy-start
  0.6 0.7 copy-done
  1.3 0.0 copy-start.1
  1.3 0.7 copy-done.1
  2.0 65.6 %shard_map.76 = (f32[4,128,128]{2,1,0:T(8,128)S(1)}, f32[8,128]{1,0:T(8,128)S(1)}, f32[4,128,128]{2,1,0:T(8,128)S(1)}) custom-call(f32[4,128,128]{2,1,0:T(8,128)} %theta_hbm.1, bf16[4,16,128,128]{3,2,1,0:T(8,128)(2,1)} %left_hbm.1, bf16[4,16,128,128]{3,2,1,0:T(8,128)(2,1)} %right_hbm.1, s32[32]{0:T(128)S(1)} %copy-done.1, s32[2,4]{1,0:T(2,128)S(1)} %bitcast.3), custom_call_target="tpu_custom_call" | custom-call | flops 1610612736 | bytes 4194304 | tf_op jit(solution)/shard_map/pallas_call | solution.py:389
  67.5 0.5 slice_bitcast_fusion
  68.0 0.7 %copy.10 = f32[4,128,128]{2,1,0:T(8,128)} copy(f32[4,128,128]{2,1,0:T(8,128)S(1)} %get-tuple-element.12) | data formatting | bytes 524288
  68.8 0.7 %copy.11 = f32[4,128,128]{2,1,0:T(8,128)} copy(f32[4,128,128]{2,1,0:T(8,128)S(1)} %get-tuple-element.14) | data formatting | bytes 524288
Async XLA Ops:
  0.6 0.7 copy-start
  1.3 0.7 copy-start.1

commit v7 on v5

--- a/solution.py
+++ b/solution.py
@@ -45,7 +45,10 @@
     core = lax.rem(s, 2)
     chip = s // 2
     sib = s + 1 - 2 * core
-    beside = [lax.rem(chip + m, n_chip) for m in range(1, n_chip)]
+    if n_chip == 4:
+        beside = [chip + 1 - 2 * lax.rem(chip, 2), lax.rem(chip + 2, 4), 3 - chip]
+    else:
+        beside = [lax.rem(chip + m, n_chip) for m in range(1, n_chip)]
     peers = [2 * c + core for c in beside]
     others = [sib] + [2 * c + 1 - core for c in beside]
     mates = [xor(z, m) for m in range(1, n_op)]
@@ -121,7 +124,7 @@
         arrived(gath[g].at[s * n_op + m], zrecv.at[m])
 
     def spread_plane(g, span, k):
-        return [move(g, s, span, psend.at[k, i], k, peer) for i, peer in enumerate(peers)]
+        return [move(g, s, span, psend.at[k, i], k, peer) for i, peer in reversed(list(enumerate(peers)))]
 
     def spread_chip(g, k):
         return [move(g, s, groups[k], psend.at[k, n_chip - 1], k, sib)]
@@ -270,10 +273,6 @@
         if not aligned:
             for i, mate in enumerate(mates):
                 rs.append(send(chunk(pb, 0, mate), rsb.at[z], rs_send.at[i], rs_recv.at[z], (s, mate)))
-        for p in range(sec_dev):
-            i = sec_dev - 1 - xor(z, p) if aligned else p
-            own = basis[step, 3 * i + 1]
-            rr = rr + fold(own * own)
         az[use, z] = dot_acc
         small = share(use)
         rsb[z] = chunk(pb, 0, z)[...]
@@ -289,6 +288,10 @@
         last = step == STEPS - 1
         if not last:
             sends += spread_plane(nxt, (0, 1), 0)
+        for p in range(sec_dev):
+            i = sec_dev - 1 - xor(z, p) if aligned else p
+            own = basis[step, 3 * i + 1]
+            rr = rr + fold(own * own)
         small += share_plane(use, jnp.concatenate([add_op(use), rr], axis=0))
         if not last:
             for m in range(1, n_op):

time: 65.9 us -> 65.1 us (0.988)
  Pallas kernels: 61.8 us -> 61 us
    pallas_call x1, Pallas kernels: 61.8 us -> 61 us  [per_device(): pl.pallas_call(functools.partial(kernel, n_sec, n_op), out_shape=(jax.Sha...]
where the time goes in v7:
time: 65.1 us; the launch traced here: 64.9 us
  Pallas kernels  61 us (94%)
  local copies, waits for them, and re-layouts  3.24 us (5%)
    pallas_call x1, Pallas kernels, per_device(): pl.pallas_call(functools.partial(kernel, n_sec, n_op), out_shape=(jax.Sha...  61 us
    unnamed x6, local copies, waits for them, and re-layouts  2.73 us

profile of v7, /device:TPU:0, one launch (start us, length us, event | category | flops | bytes accessed | tf_op | source)
XLA Modules:
  0.0 64.9 jit_solution(16914152567981495855)
XLA Ops:
  0.6 0.0 copy-start
  0.6 0.7 %copy-done = s32[4,2]{0,1:T(2,128)S(1)} copy-done((s32[4,2]{0,1:T(2,128)S(1)}, s32[4,2]{0,1:T(2,128)}, u32[]{:S(2)}) %copy-start) | copy-done | bytes 56
  1.3 0.0 copy-start.1
  1.3 0.7 %copy-done.1 = s32[32]{0:T(128)S(1)} copy-done((s32[32]{0:T(128)S(1)}, s32[32]{0:T(128)}, u32[]{:S(2)}) %copy-start.1) | copy-done | bytes 152
  2.0 61.0 %shard_map.76 = (f32[4,128,128]{2,1,0:T(8,128)S(1)}, f32[8,128]{1,0:T(8,128)S(1)}, f32[4,128,128]{2,1,0:T(8,128)S(1)}) custom-call(f32[4,128,128]{2,1,0:T(8,128)} %theta_hbm.1, bf16[4,16,128,128]{3,2,1,0:T(8,128)(2,1)} %left_hbm.1, bf16[4,16,128,128]{3,2,1,0:T(8,128)(2,1)} %right_hbm.1, s32[32]{0:T(128)S(1)} %copy-done.1, s32[2,4]{1,0:T(2,128)S(1)} %bitcast.3), custom_call_target="tpu_custom_call" | custom-call | flops 1610612736 | bytes 4194304 | tf_op jit(solution)/shard_map/pallas_call | solution.py:361
  63.0 0.5 slice_bitcast_fusion
  63.5 0.7 %copy.10 = f32[4,128,128]{2,1,0:T(8,128)} copy(f32[4,128,128]{2,1,0:T(8,128)S(1)} %get-tuple-element.12) | data formatting | bytes 524288
  64.2 0.7 %copy.11 = f32[4,128,128]{2,1,0:T(8,128)} copy(f32[4,128,128]{2,1,0:T(8,128)S(1)} %get-tuple-element.14) | data formatting | bytes 524288
Async XLA Ops:
  0.6 0.7 %copy-start = (s32[4,2]{0,1:T(2,128)S(1)}, s32[4,2]{0,1:T(2,128)}, u32[]{:S(2)}) copy-start(s32[4,2]{0,1:T(2,128)} %param.9) | copy-start | bytes 100
  1.3 0.7 %copy-start.1 = (s32[32]{0:T(128)S(1)}, s32[32]{0:T(128)}, u32[]{:S(2)}) copy-start(s32[32]{0:T(128)} %perm_ref.1) | copy-start | bytes 388
